TPU v7x, 128 devices: a whole 4x4x4 slice. The times are simulated.
128 devices in a mesh: slab: 16 (over x, z), member: 8 (over y, core).
Axes of the slice: x: 4, y: 4, z: 4, core: 2. Of those that a mesh axis runs over, the one named last changes fastest.
Arguments:
- embeddings: bfloat16 [131072, 768], P(('slab', 'member')), may hold values from -6 to 6
- cluster_ids: int32 [131072], P(('slab', 'member')), may hold values from 0 to 63, never falling along the last dimension, each value on 1 to 4097 neighbouring positions
- keep_mask: int32 [131072], P(('slab', 'member')), may hold values 0 or 1
Outputs:
- highest: float32 [131072], P(('slab', 'member'))
Inputs may be any that keep to these rules, and one draw needn't show every extreme that they name: `cluster_ids`: never falling along the rows; each cluster is a run of 1 to 4097 consecutive rows, and some cluster has exactly 4097 rows.
All inputs are finite; a program needn't handle non-finite values. No bound on the sum of `keep_mask` on one device may be relied on, other than what follows from the above.
Results may differ from a plain program's by a relative error of at most 0.0013.
Values may be sent and summed in bfloat16 or wider, within the bound.
A program may use at most 64 MiB of HBM per device.

v0:
```python
import jax
import jax.numpy as jnp
from jax import lax
from jax.sharding import PartitionSpec as P

REACH = 4


def passed_along(value, axis, by):
    size = lax.axis_size(axis)
    pairs = [(i, i + by) for i in range(size) if 0 <= i + by < size]
    return lax.ppermute(value, axis, pairs)


def tile_scores(own_rows, other_rows):
    return jnp.dot(own_rows, other_rows.T, preferred_element_type=jnp.float32)


def shards(embeddings, cluster_ids, keep_mask):
    row_count = embeddings.shape[0]
    values = embeddings.astype(jnp.float32)
    unit_rows = (
        values * lax.rsqrt(jnp.sum(values * values, axis=1, keepdims=True) + 1e-06)
    ).astype(jnp.bfloat16)
    labels = jnp.where(keep_mask == 1, cluster_ids, -1)
    row_tags = jnp.stack([cluster_ids, labels])
    position = lax.axis_index(("slab", "member"))
    device_count = lax.axis_size(("slab", "member"))
    filler = jnp.full((row_count,), -1.0, jnp.float32)
    scores = tile_scores(unit_rows, unit_rows)
    matches = (cluster_ids[:, None] == labels[None, :]) & jnp.logical_not(
        jnp.eye(row_count, dtype=bool)
    )
    highest = jnp.max(jnp.where(matches, scores, -1.0), axis=1)

    def row_side(other_rows, other_tags, shares):

        def compute(operands):
            found = tile_scores(unit_rows, other_rows)
            hits = cluster_ids[:, None] == other_tags[1][None, :]
            return jnp.max(jnp.where(hits, found, -1.0), axis=1)

        return lax.cond(shares, compute, lambda operands: filler, 0)

    for offset in range(1, REACH + 1):
        lower_rows, lower_tags = passed_along((unit_rows, row_tags), ("slab", "member"), offset)
        lower_shares = (position >= offset) & (lower_tags[0][-1] == cluster_ids[0])
        upper_rows, upper_tags = passed_along((unit_rows, row_tags), ("slab", "member"), -offset)
        upper_shares = (position + offset < device_count) & (upper_tags[0][0] == cluster_ids[-1])
        highest = jnp.maximum(highest, row_side(lower_rows, lower_tags, lower_shares))
        highest = jnp.maximum(highest, row_side(upper_rows, upper_tags, upper_shares))
    return highest


def solution(mesh):
    placed = (P(("slab", "member"), None), P(("slab", "member")), P(("slab", "member")))
    return jax.shard_map(
        shards, mesh=mesh, in_specs=placed, out_specs=P(("slab", "member")), check_vma=False
    )
```

profile of v0, /device:TPU:4, one launch (start us, length us, event | category | flops | bytes accessed | tf_op | source)
XLA Modules:
  0.0 243.2 jit_solution(10911450689937236814)
XLA Ops:
  0.0 1.9 fusion.2
  1.9 0.0 copy-start.1
  1.9 0.0 copy-start.2
  2.0 0.3 fusion.3
  2.3 8.5 %collective-permute-start.15 = (bf16[1024,768]{1,0:T(8,128)(2,1)S(1)}, bf16[1024,768]{1,0:T(8,128)(2,1)S(1)}, u32[]{:S(2)}, u32[]{:S(2)}) collective-permute-start(bf16[1024,768]{1,0:T(8,128)(2,1)S(1)} %fusion.3), channel_id=1, source_target_pairs={{4,0},{5,1},{6,2},{7,3},{8,4},{9,5},{10,6},{11,7},{12,8},{13,9},{1... | collective-permute-start | bytes 4718600 | tf_op jit(solution)/shard_map/ppermute | solution.py:12
  10.8 1.9 collective-permute-start.13
  12.8 7.3 %collective-permute-start.11 = (bf16[1024,768]{1,0:T(8,128)(2,1)S(1)}, bf16[1024,768]{1,0:T(8,128)(2,1)S(1)}, u32[]{:S(2)}, u32[]{:S(2)}) collective-permute-start(bf16[1024,768]{1,0:T(8,128)(2,1)S(1)} %fusion.3), channel_id=1, source_target_pairs={{3,0},{4,1},{5,2},{6,3},{7,4},{8,5},{9,6},{10,7},{11,8},{12,9},{13... | collective-permute-start | bytes 4718600 | tf_op jit(solution)/shard_map/ppermute | solution.py:12
  20.1 3.0 %collective-permute-start.14 = (s32[2,1024]{1,0:T(2,128)S(1)}, s32[2,1024]{1,0:T(2,128)S(1)}, u32[]{:S(2)}, u32[]{:S(2)}) collective-permute-start(s32[2,1024]{1,0:T(2,128)S(1)} %pad_add_fusion), channel_id=1, source_target_pairs={{4,0},{5,1},{6,2},{7,3},{8,4},{9,5},{10,6},{11,7},{12,8},{13,9},{1... | collective-permute-start | bytes 24584 | tf_op jit(solution)/shard_map/ppermute | solution.py:12
  23.2 4.3 %collective-permute-start.12 = (s32[2,1024]{1,0:T(2,128)S(1)}, s32[2,1024]{1,0:T(2,128)S(1)}, u32[]{:S(2)}, u32[]{:S(2)}) collective-permute-start(s32[2,1024]{1,0:T(2,128)S(1)} %pad_add_fusion), channel_id=1, source_target_pairs={{0,4},{1,5},{2,6},{3,7},{4,8},{5,9},{6,10},{7,11},{8,12},{9,13},{1... | collective-permute-start | bytes 24584 | tf_op jit(solution)/shard_map/ppermute | solution.py:12
  27.5 65.1 %collective-permute-done.14 = s32[2,1024]{1,0:T(2,128)S(1)} collective-permute-done((s32[2,1024]{1,0:T(2,128)S(1)}, s32[2,1024]{1,0:T(2,128)S(1)}, u32[]{:S(2)}, u32[]{:S(2)}) %collective-permute-start.14) | collective-permute-done | bytes 8224 | tf_op jit(solution)/shard_map/ppermute | solution.py:12
  92.6 1.9 collective-permute-start.10
  94.6 1.8 collective-permute-done.12
  96.3 36.0 %collective-permute-start.8 = (s32[2,1024]{1,0:T(2,128)S(1)}, s32[2,1024]{1,0:T(2,128)S(1)}, u32[]{:S(2)}, u32[]{:S(2)}) collective-permute-start(s32[2,1024]{1,0:T(2,128)S(1)} %pad_add_fusion), channel_id=1, source_target_pairs={{0,3},{1,4},{2,5},{3,6},{4,7},{5,8},{6,9},{7,10},{8,11},{9,12},{10... | collective-permute-start | bytes 24584 | tf_op jit(solution)/shard_map/ppermute | solution.py:12
  132.3 0.0 collective-permute-done.10
  132.4 1.9 collective-permute-start.6
  134.3 0.0 collective-permute-done.8
  134.3 3.9 %collective-permute-start.4 = (s32[2,1024]{1,0:T(2,128)S(1)}, s32[2,1024]{1,0:T(2,128)S(1)}, u32[]{:S(2)}, u32[]{:S(2)}) collective-permute-start(s32[2,1024]{1,0:T(2,128)S(1)} %pad_add_fusion), channel_id=1, source_target_pairs={{0,2},{1,3},{2,4},{3,5},{4,6},{5,7},{6,8},{7,9},{8,10},{9,11},{10,... | collective-permute-start | bytes 24584 | tf_op jit(solution)/shard_map/ppermute | solution.py:12
  138.2 0.0 collective-permute-done.6
  138.2 1.9 collective-permute-start.2
  140.2 3.9 %collective-permute-done.4 = s32[2,1024]{1,0:T(2,128)S(1)} collective-permute-done((s32[2,1024]{1,0:T(2,128)S(1)}, s32[2,1024]{1,0:T(2,128)S(1)}, u32[]{:S(2)}, u32[]{:S(2)}) %collective-permute-start.4) | collective-permute-done | bytes 8224 | tf_op jit(solution)/shard_map/ppermute | solution.py:12
  144.1 1.9 collective-permute-start
  146.0 0.0 collective-permute-done.2
  146.0 2.0 collective-permute-start.9
  148.0 5.2 %collective-permute-done = s32[2,1024]{1,0:T(2,128)S(1)} collective-permute-done((s32[2,1024]{1,0:T(2,128)S(1)}, s32[2,1024]{1,0:T(2,128)S(1)}, u32[]{:S(2)}, u32[]{:S(2)}) %collective-permute-start) | collective-permute-done | bytes 8224 | tf_op jit(solution)/shard_map/ppermute | solution.py:12
  153.2 1.9 collective-permute-start.7
  155.2 0.0 collective-permute-done.15
  155.2 3.9 %collective-permute-start.5 = (bf16[1024,768]{1,0:T(8,128)(2,1)S(1)}, bf16[1024,768]{1,0:T(8,128)(2,1)}, u32[]{:S(2)}, u32[]{:S(2)}) collective-permute-start(bf16[1024,768]{1,0:T(8,128)(2,1)S(1)} %fusion.3), channel_id=1, source_target_pairs={{0,2},{1,3},{2,4},{3,5},{4,6},{5,7},{6,8},{7,9},{8,10},{9,11},{10,... | collective-permute-start | bytes 4718600 | tf_op jit(solution)/shard_map/ppermute | solution.py:12
  159.1 0.0 collective-permute-done.13
  159.1 6.2 %collective-permute-start.3 = (bf16[1024,768]{1,0:T(8,128)(2,1)S(1)}, bf16[1024,768]{1,0:T(8,128)(2,1)}, u32[]{:S(2)}, u32[]{:S(2)}) collective-permute-start(bf16[1024,768]{1,0:T(8,128)(2,1)S(1)} %fusion.3), channel_id=1, source_target_pairs={{1,0},{2,1},{3,2},{4,3},{5,4},{6,5},{7,6},{8,7},{9,8},{10,9},{11,1... | collective-permute-start | bytes 4718600 | tf_op jit(solution)/shard_map/ppermute | solution.py:12
  165.4 0.0 collective-permute-done.11
  165.4 1.1 copy-done.3
  166.5 1.9 collective-permute-start.1
  168.5 0.6 fusion.4
  169.1 2.0 select_reduce_fusion.8
  171.1 0.5 slice.101
  172.9 0.6 slice.100
  174.6 0.5 slice.99
  176.4 0.6 slice.98
  178.2 0.5 slice.97
  180.0 0.6 slice.96
  181.9 0.6 slice.95
  183.8 0.7 slice.94
  185.7 3.3 %conditional.15 = (f32[1024]{0:T(1024)S(1)}) conditional(s32[]{:T(128)} %convert_element_type.39, () %tuple.67, (s32[1024]{0:T(1024)S(1)}, s32[2,1024]{1,0:T(2,128)S(1)}, bf16[1024,768]{1,0:T(8,128)(2,1)S(1)}, bf16[1024,768]{1,0:T(8,128)(2,1)}) %tuple.96), branch_computations={%region_23.24_spmd, %region_24.26_spmd} | conditional | flops 1613757440 | bytes 3166216 | solution.py:43
  185.7 3.2 %select_reduce_fusion.7 = f32[1024]{0:T(1024)S(1)} fusion(s32[1024]{0:T(1024)S(1)} %get-tuple-element.121, s32[1024]{0:T(1024)S(1)} %bitcast.40, bf16[1024,768]{1,0:T(8,128)(2,1)S(1)} %get-tuple-element.123, bf16[1024,768]{1,0:T(8,128)(2,1)} %get-tuple-element.124), kind=kOutput, calls=%fused_computation.7 | convolution fusion | flops 1613757440 | bytes 3158016 | tf_op jit(solution)/shard_map/cond/branch_1_fun/dot_general | solution.py:16
  189.0 3.3 %conditional.14 = (f32[1024]{0:T(1024)S(1)}) conditional(s32[]{:T(128)} %convert_element_type.38, () %tuple.65, (s32[1024]{0:T(1024)S(1)}, s32[2,1024]{1,0:T(2,128)S(1)}, bf16[1024,768]{1,0:T(8,128)(2,1)S(1)}, bf16[1024,768]{1,0:T(8,128)(2,1)}) %tuple.95), branch_computations={%region_20.21_spmd, %region_21.23_spmd} | conditional | flops 1613757440 | bytes 3166216 | solution.py:43
  189.0 3.2 %select_reduce_fusion.6 = f32[1024]{0:T(1024)S(1)} fusion(s32[1024]{0:T(1024)S(1)} %get-tuple-element.117, s32[1024]{0:T(1024)S(1)} %bitcast.41, bf16[1024,768]{1,0:T(8,128)(2,1)S(1)} %get-tuple-element.119, bf16[1024,768]{1,0:T(8,128)(2,1)} %get-tuple-element.120), kind=kOutput, calls=%fused_computation.6 | convolution fusion | flops 1613757440 | bytes 3158016 | tf_op jit(solution)/shard_map/cond/branch_1_fun/dot_general | solution.py:16
  192.2 3.3 %conditional.13 = (f32[1024]{0:T(1024)S(1)}) conditional(s32[]{:T(128)} %convert_element_type.37, () %tuple.63, (s32[1024]{0:T(1024)S(1)}, s32[2,1024]{1,0:T(2,128)S(1)}, bf16[1024,768]{1,0:T(8,128)(2,1)S(1)}, bf16[1024,768]{1,0:T(8,128)(2,1)}) %tuple.94), branch_computations={%region_17.18_spmd, %region_18.20_spmd} | conditional | flops 1613757440 | bytes 3166216 | solution.py:43
  192.3 3.2 %select_reduce_fusion.5 = f32[1024]{0:T(1024)S(1)} fusion(s32[1024]{0:T(1024)S(1)} %get-tuple-element.113, s32[1024]{0:T(1024)S(1)} %bitcast.42, bf16[1024,768]{1,0:T(8,128)(2,1)S(1)} %get-tuple-element.115, bf16[1024,768]{1,0:T(8,128)(2,1)} %get-tuple-element.116), kind=kOutput, calls=%fused_computation.5 | convolution fusion | flops 1613757440 | bytes 3158016 | tf_op jit(solution)/shard_map/cond/branch_1_fun/dot_general | solution.py:16
  195.5 0.0 collective-permute-done.9
  195.5 3.3 %conditional.12 = (f32[1024]{0:T(1024)S(1)}) conditional(s32[]{:T(128)} %convert_element_type.36, () %tuple.61, (s32[1024]{0:T(1024)S(1)}, s32[2,1024]{1,0:T(2,128)S(1)}, bf16[1024,768]{1,0:T(8,128)(2,1)S(1)}, bf16[1024,768]{1,0:T(8,128)(2,1)}) %tuple.89), branch_computations={%region_14.15_spmd, %region_15.17_spmd} | conditional | flops 1613757440 | bytes 3166216 | solution.py:43
  195.6 3.2 %select_reduce_fusion.4 = f32[1024]{0:T(1024)S(1)} fusion(s32[1024]{0:T(1024)S(1)} %get-tuple-element.109, s32[1024]{0:T(1024)S(1)} %bitcast.43, bf16[1024,768]{1,0:T(8,128)(2,1)S(1)} %get-tuple-element.111, bf16[1024,768]{1,0:T(8,128)(2,1)} %get-tuple-element.112), kind=kOutput, calls=%fused_computation.4 | convolution fusion | flops 1613757440 | bytes 3158016 | tf_op jit(solution)/shard_map/cond/branch_1_fun/dot_general | solution.py:16
  198.8 0.3 collective-permute-done.7
  199.1 3.2 %conditional.11 = (f32[1024]{0:T(1024)S(1)}) conditional(s32[]{:T(128)} %convert_element_type.35, () %tuple.59, (s32[1024]{0:T(1024)S(1)}, s32[2,1024]{1,0:T(2,128)S(1)}, bf16[1024,768]{1,0:T(8,128)(2,1)S(1)}, bf16[1024,768]{1,0:T(8,128)(2,1)}) %tuple.90), branch_computations={%region_11.12_spmd, %region_12.14_spmd} | conditional | flops 1613757440 | bytes 3166216 | solution.py:43
  199.1 3.2 %select_reduce_fusion.3 = f32[1024]{0:T(1024)S(1)} fusion(s32[1024]{0:T(1024)S(1)} %get-tuple-element.105, s32[1024]{0:T(1024)S(1)} %bitcast.44, bf16[1024,768]{1,0:T(8,128)(2,1)S(1)} %get-tuple-element.107, bf16[1024,768]{1,0:T(8,128)(2,1)} %get-tuple-element.108), kind=kOutput, calls=%fused_computation.3 | convolution fusion | flops 1613757440 | bytes 3158016 | tf_op jit(solution)/shard_map/cond/branch_1_fun/dot_general | solution.py:16
  202.3 20.3 %collective-permute-done.5 = bf16[1024,768]{1,0:T(8,128)(2,1)} collective-permute-done((bf16[1024,768]{1,0:T(8,128)(2,1)S(1)}, bf16[1024,768]{1,0:T(8,128)(2,1)}, u32[]{:S(2)}, u32[]{:S(2)}) %collective-permute-start.5) | collective-permute-done | bytes 1572896 | tf_op jit(solution)/shard_map/ppermute | solution.py:12
  222.7 3.2 %conditional.10 = (f32[1024]{0:T(1024)S(1)}) conditional(s32[]{:T(128)} %convert_element_type.34, () %tuple.57, (s32[1024]{0:T(1024)S(1)}, s32[2,1024]{1,0:T(2,128)S(1)}, bf16[1024,768]{1,0:T(8,128)(2,1)S(1)}, bf16[1024,768]{1,0:T(8,128)(2,1)}) %tuple.91), branch_computations={%region_8.9_spmd, %region_9.11_spmd} | conditional | flops 1613757440 | bytes 3166216 | solution.py:43
  222.7 3.2 %select_reduce_fusion.2 = f32[1024]{0:T(1024)S(1)} fusion(s32[1024]{0:T(1024)S(1)} %get-tuple-element.101, s32[1024]{0:T(1024)S(1)} %bitcast.45, bf16[1024,768]{1,0:T(8,128)(2,1)S(1)} %get-tuple-element.103, bf16[1024,768]{1,0:T(8,128)(2,1)} %get-tuple-element.104), kind=kOutput, calls=%fused_computation.2 | convolution fusion | flops 1613757440 | bytes 3158016 | tf_op jit(solution)/shard_map/cond/branch_1_fun/dot_general | solution.py:16
  225.9 0.0 collective-permute-done.3
  225.9 3.5 %conditional.9 = (f32[1024]{0:T(1024)S(1)}) conditional(s32[]{:T(128)} %convert_element_type.33, () %tuple.55, (s32[1024]{0:T(1024)S(1)}, s32[2,1024]{1,0:T(2,128)S(1)}, bf16[1024,768]{1,0:T(8,128)(2,1)S(1)}, bf16[1024,768]{1,0:T(8,128)(2,1)}) %tuple.92), branch_computations={%region_5.6_spmd, %region_6.8_spmd} | conditional | flops 1613757440 | bytes 3166216 | solution.py:43
  226.1 3.2 %select_reduce_fusion.1 = f32[1024]{0:T(1024)S(1)} fusion(s32[1024]{0:T(1024)S(1)} %get-tuple-element.90, s32[1024]{0:T(1024)S(1)} %bitcast.46, bf16[1024,768]{1,0:T(8,128)(2,1)S(1)} %get-tuple-element.98, bf16[1024,768]{1,0:T(8,128)(2,1)} %get-tuple-element.100), kind=kOutput, calls=%fused_computation.1 | convolution fusion | flops 1613757440 | bytes 3158016 | tf_op jit(solution)/shard_map/cond/branch_1_fun/dot_general | solution.py:16
  229.4 11.4 %collective-permute-done.1 = bf16[1024,768]{1,0:T(8,128)(2,1)S(1)} collective-permute-done((bf16[1024,768]{1,0:T(8,128)(2,1)S(1)}, bf16[1024,768]{1,0:T(8,128)(2,1)S(1)}, u32[]{:S(2)}, u32[]{:S(2)}) %collective-permute-start.1) | collective-permute-done | bytes 1572896 | tf_op jit(solution)/shard_map/ppermute | solution.py:12
  240.8 1.8 conditional.8
  240.8 1.8 select_reduce_fusion
  242.6 0.6 maximum_maximum_fusion
  (20 shorter events, 0.1 us)
Async XLA Ops:
  0.0 1.9 copy-start
  1.9 18.2 %copy-start.1 = (s32[1024]{0:T(1024)S(1)}, s32[1024]{0:T(1024)}, u32[]{:S(2)}) copy-start(s32[1024]{0:T(1024)} %param.20) | copy-start | bytes 12292
  1.9 18.2 %copy-start.2 = (s32[1024]{0:T(1024)S(1)}, s32[1024]{0:T(1024)}, u32[]{:S(2)}) copy-start(s32[1024]{0:T(1024)} %param.21) | copy-start | bytes 12292
  2.3 152.9 %collective-permute-start.15 = (bf16[1024,768]{1,0:T(8,128)(2,1)S(1)}, bf16[1024,768]{1,0:T(8,128)(2,1)S(1)}, u32[]{:S(2)}, u32[]{:S(2)}) collective-permute-start(bf16[1024,768]{1,0:T(8,128)(2,1)S(1)} %fusion.3), channel_id=1, source_target_pairs={{4,0},{5,1},{6,2},{7,3},{8,4},{9,5},{10,6},{11,7},{12,8},{13,9},{1... | collective-permute-start | bytes 4718600 | tf_op jit(solution)/shard_map/ppermute | solution.py:12
  10.8 148.3 %collective-permute-start.13 = (bf16[1024,768]{1,0:T(8,128)(2,1)S(1)}, bf16[1024,768]{1,0:T(8,128)(2,1)S(1)}, u32[]{:S(2)}, u32[]{:S(2)}) collective-permute-start(bf16[1024,768]{1,0:T(8,128)(2,1)S(1)} %fusion.3), channel_id=1, source_target_pairs={{0,4},{1,5},{2,6},{3,7},{4,8},{5,9},{6,10},{7,11},{8,12},{9,13},{1... | collective-permute-start | bytes 4718600 | tf_op jit(solution)/shard_map/ppermute | solution.py:12
  12.8 152.6 %collective-permute-start.11 = (bf16[1024,768]{1,0:T(8,128)(2,1)S(1)}, bf16[1024,768]{1,0:T(8,128)(2,1)S(1)}, u32[]{:S(2)}, u32[]{:S(2)}) collective-permute-start(bf16[1024,768]{1,0:T(8,128)(2,1)S(1)} %fusion.3), channel_id=1, source_target_pairs={{3,0},{4,1},{5,2},{6,3},{7,4},{8,5},{9,6},{10,7},{11,8},{12,9},{13... | collective-permute-start | bytes 4718600 | tf_op jit(solution)/shard_map/ppermute | solution.py:12
  20.1 72.5 %collective-permute-start.14 = (s32[2,1024]{1,0:T(2,128)S(1)}, s32[2,1024]{1,0:T(2,128)S(1)}, u32[]{:S(2)}, u32[]{:S(2)}) collective-permute-start(s32[2,1024]{1,0:T(2,128)S(1)} %pad_add_fusion), channel_id=1, source_target_pairs={{4,0},{5,1},{6,2},{7,3},{8,4},{9,5},{10,6},{11,7},{12,8},{13,9},{1... | collective-permute-start | bytes 24584 | tf_op jit(solution)/shard_map/ppermute | solution.py:12
  23.2 73.1 %collective-permute-start.12 = (s32[2,1024]{1,0:T(2,128)S(1)}, s32[2,1024]{1,0:T(2,128)S(1)}, u32[]{:S(2)}, u32[]{:S(2)}) collective-permute-start(s32[2,1024]{1,0:T(2,128)S(1)} %pad_add_fusion), channel_id=1, source_target_pairs={{0,4},{1,5},{2,6},{3,7},{4,8},{5,9},{6,10},{7,11},{8,12},{9,13},{1... | collective-permute-start | bytes 24584 | tf_op jit(solution)/shard_map/ppermute | solution.py:12
  92.6 39.7 %collective-permute-start.10 = (s32[2,1024]{1,0:T(2,128)S(1)}, s32[2,1024]{1,0:T(2,128)S(1)}, u32[]{:S(2)}, u32[]{:S(2)}) collective-permute-start(s32[2,1024]{1,0:T(2,128)S(1)} %pad_add_fusion), channel_id=1, source_target_pairs={{3,0},{4,1},{5,2},{6,3},{7,4},{8,5},{9,6},{10,7},{11,8},{12,9},{13... | collective-permute-start | bytes 24584 | tf_op jit(solution)/shard_map/ppermute | solution.py:12
  96.3 38.0 %collective-permute-start.8 = (s32[2,1024]{1,0:T(2,128)S(1)}, s32[2,1024]{1,0:T(2,128)S(1)}, u32[]{:S(2)}, u32[]{:S(2)}) collective-permute-start(s32[2,1024]{1,0:T(2,128)S(1)} %pad_add_fusion), channel_id=1, source_target_pairs={{0,3},{1,4},{2,5},{3,6},{4,7},{5,8},{6,9},{7,10},{8,11},{9,12},{10... | collective-permute-start | bytes 24584 | tf_op jit(solution)/shard_map/ppermute | solution.py:12
  132.4 5.9 %collective-permute-start.6 = (s32[2,1024]{1,0:T(2,128)S(1)}, s32[2,1024]{1,0:T(2,128)S(1)}, u32[]{:S(2)}, u32[]{:S(2)}) collective-permute-start(s32[2,1024]{1,0:T(2,128)S(1)} %pad_add_fusion), channel_id=1, source_target_pairs={{2,0},{3,1},{4,2},{5,3},{6,4},{7,5},{8,6},{9,7},{10,8},{11,9},{12,... | collective-permute-start | bytes 24584 | tf_op jit(solution)/shard_map/ppermute | solution.py:12
  134.3 9.8 %collective-permute-start.4 = (s32[2,1024]{1,0:T(2,128)S(1)}, s32[2,1024]{1,0:T(2,128)S(1)}, u32[]{:S(2)}, u32[]{:S(2)}) collective-permute-start(s32[2,1024]{1,0:T(2,128)S(1)} %pad_add_fusion), channel_id=1, source_target_pairs={{0,2},{1,3},{2,4},{3,5},{4,6},{5,7},{6,8},{7,9},{8,10},{9,11},{10,... | collective-permute-start | bytes 24584 | tf_op jit(solution)/shard_map/ppermute | solution.py:12
  138.2 7.7 %collective-permute-start.2 = (s32[2,1024]{1,0:T(2,128)S(1)}, s32[2,1024]{1,0:T(2,128)S(1)}, u32[]{:S(2)}, u32[]{:S(2)}) collective-permute-start(s32[2,1024]{1,0:T(2,128)S(1)} %pad_add_fusion), channel_id=1, source_target_pairs={{1,0},{2,1},{3,2},{4,3},{5,4},{6,5},{7,6},{8,7},{9,8},{10,9},{11,1... | collective-permute-start | bytes 24584 | tf_op jit(solution)/shard_map/ppermute | solution.py:12
  144.1 9.2 %collective-permute-start = (s32[2,1024]{1,0:T(2,128)S(1)}, s32[2,1024]{1,0:T(2,128)S(1)}, u32[]{:S(2)}, u32[]{:S(2)}) collective-permute-start(s32[2,1024]{1,0:T(2,128)S(1)} %pad_add_fusion), channel_id=1, source_target_pairs={{0,1},{1,2},{2,3},{3,4},{4,5},{5,6},{6,7},{7,8},{8,9},{9,10},{10,1... | collective-permute-start | bytes 24584 | tf_op jit(solution)/shard_map/ppermute | solution.py:12
  146.0 49.5 %collective-permute-start.9 = (bf16[1024,768]{1,0:T(8,128)(2,1)S(1)}, bf16[1024,768]{1,0:T(8,128)(2,1)}, u32[]{:S(2)}, u32[]{:S(2)}) collective-permute-start(bf16[1024,768]{1,0:T(8,128)(2,1)S(1)} %fusion.3), channel_id=1, source_target_pairs={{0,3},{1,4},{2,5},{3,6},{4,7},{5,8},{6,9},{7,10},{8,11},{9,12},{10... | collective-permute-start | bytes 4718600 | tf_op jit(solution)/shard_map/ppermute | solution.py:12
  153.2 45.9 %collective-permute-start.7 = (bf16[1024,768]{1,0:T(8,128)(2,1)S(1)}, bf16[1024,768]{1,0:T(8,128)(2,1)}, u32[]{:S(2)}, u32[]{:S(2)}) collective-permute-start(bf16[1024,768]{1,0:T(8,128)(2,1)S(1)} %fusion.3), channel_id=1, source_target_pairs={{2,0},{3,1},{4,2},{5,3},{6,4},{7,5},{8,6},{9,7},{10,8},{11,9},{12,... | collective-permute-start | bytes 4718600 | tf_op jit(solution)/shard_map/ppermute | solution.py:12
  155.2 13.3 %copy-start.5 = (bf16[1024,768]{1,0:T(8,128)(2,1)}, bf16[1024,768]{1,0:T(8,128)(2,1)S(1)}, u32[]{:S(2)}) copy-start(bf16[1024,768]{1,0:T(8,128)(2,1)S(1)} %collective-permute-done.15) | copy-start | bytes 4718596
  155.2 67.5 %collective-permute-start.5 = (bf16[1024,768]{1,0:T(8,128)(2,1)S(1)}, bf16[1024,768]{1,0:T(8,128)(2,1)}, u32[]{:S(2)}, u32[]{:S(2)}) collective-permute-start(bf16[1024,768]{1,0:T(8,128)(2,1)S(1)} %fusion.3), channel_id=1, source_target_pairs={{0,2},{1,3},{2,4},{3,5},{4,6},{5,7},{6,8},{7,9},{8,10},{9,11},{10,... | collective-permute-start | bytes 4718600 | tf_op jit(solution)/shard_map/ppermute | solution.py:12
  159.1 9.3 %copy-start.4 = (bf16[1024,768]{1,0:T(8,128)(2,1)}, bf16[1024,768]{1,0:T(8,128)(2,1)S(1)}, u32[]{:S(2)}) copy-start(bf16[1024,768]{1,0:T(8,128)(2,1)S(1)} %collective-permute-done.13) | copy-start | bytes 4718596
  159.1 66.8 %collective-permute-start.3 = (bf16[1024,768]{1,0:T(8,128)(2,1)S(1)}, bf16[1024,768]{1,0:T(8,128)(2,1)}, u32[]{:S(2)}, u32[]{:S(2)}) collective-permute-start(bf16[1024,768]{1,0:T(8,128)(2,1)S(1)} %fusion.3), channel_id=1, source_target_pairs={{1,0},{2,1},{3,2},{4,3},{5,4},{6,5},{7,6},{8,7},{9,8},{10,9},{11,1... | collective-permute-start | bytes 4718600 | tf_op jit(solution)/shard_map/ppermute | solution.py:12
  165.4 1.2 copy-start.3
  166.5 74.2 %collective-permute-start.1 = (bf16[1024,768]{1,0:T(8,128)(2,1)S(1)}, bf16[1024,768]{1,0:T(8,128)(2,1)S(1)}, u32[]{:S(2)}, u32[]{:S(2)}) collective-permute-start(bf16[1024,768]{1,0:T(8,128)(2,1)S(1)} %fusion.3), channel_id=1, source_target_pairs={{0,1},{1,2},{2,3},{3,4},{4,5},{5,6},{6,7},{7,8},{8,9},{9,10},{10,1... | collective-permute-start | bytes 4718600 | tf_op jit(solution)/shard_map/ppermute | solution.py:12
where the time goes:
time: 244 us; the launch traced here: 243 us
  waiting for transfers between devices  108 us (44%)
  starting transfers between devices  88.7 us (36%)
  matrix products  26.5 us (11%)
  between operations  10.3 us (4%)
  local copies, waits for them, and re-layouts  6.49 us (3%)
  other arithmetic  2.85 us (1%)
    ppermute x16, waiting for transfers between devices, passed_along(): return lax.ppermute(value, axis, pairs)  108 us
    ppermute x16, starting transfers between devices, passed_along(): return lax.ppermute(value, axis, pairs)  88.7 us
    dot_general x9, matrix products, tile_scores(): return jnp.dot(own_rows, other_rows.T, preferred_element_type=jnp.float32)  26.5 us
  transfers between devices with their start and end apart: 16, of which 7 were waited for; matrix products, arithmetic and copies ran while one was open for 12% of the time, Pallas kernels for 0%

commit v1 on v0

v1 whole, which is shorter than its diff:
```python
import functools

import jax
import jax.numpy as jnp
from jax import lax
from jax.experimental import pallas as pl
from jax.experimental.pallas import tpu as pltpu
from jax.sharding import PartitionSpec as P

MESH = pl.DeviceIdType.MESH
OWN, A, B, C = 0, 1, 2, 3
LANES = 128
OUT = -4.0


def kernel(n_slab, n_member, x_ref, ids_ref, keep_ref, out_ref, raw, blk, tags, pres, qacc, msg, got,
           load_sem, send_sem, recv_sem, tag_send, tag_recv, msg_send, msg_recv):
    rows, width = raw.shape
    chunks = rows // LANES
    count = n_slab * n_member
    slab, member = lax.axis_index("slab"), lax.axis_index("member")
    core = lax.rem(member, 2)
    place = slab * n_member + member

    def device(at):
        at = lax.rem(at + count, count)
        return (lax.div(at, n_member), lax.rem(at, n_member))

    first = device(place - 2 + 4 * core)
    second = device(place + 2 - 4 * core)
    sibling = (slab, member + 1 - 2 * core)
    above, below = device(place + 1), device(place - 1)

    barrier = pltpu.get_barrier_semaphore()
    for other in (first, second, above, below):
        pl.semaphore_signal(barrier, inc=1, device_id=other, device_id_type=MESH)

    def part(t):
        return pl.ds(pl.multiple_of(t * LANES, LANES), LANES)

    def load(t):
        return pltpu.make_async_copy(x_ref.at[part(t)], raw.at[part(t)], load_sem.at[t])

    def send(src_slot, dst_slot, t, target):
        return pltpu.make_async_remote_copy(
            src_ref=blk.at[src_slot, part(t)], dst_ref=blk.at[dst_slot, part(t)],
            send_sem=send_sem.at[dst_slot, t], recv_sem=recv_sem.at[dst_slot, t],
            device_id=target, device_id_type=MESH)

    def send_tags(src_slot, dst_slot, target):
        return pltpu.make_async_remote_copy(
            src_ref=tags.at[src_slot], dst_ref=tags.at[dst_slot], send_sem=tag_send.at[dst_slot],
            recv_sem=tag_recv.at[dst_slot], device_id=target, device_id_type=MESH)

    for t in range(chunks):
        load(t).start()
    tags[OWN, 0:chunks] = ids_ref[...]
    tags[OWN, chunks:2 * chunks] = jnp.where(keep_ref[...] == 1, ids_ref[...], -1)
    pres[...] = jnp.full(pres.shape, OUT, jnp.float32)
    qacc[...] = jnp.full(qacc.shape, OUT, jnp.float32)

    def normalise(t):
        load(t).wait()
        values = raw[part(t), :].astype(jnp.float32)
        scale = lax.rsqrt(jnp.sum(values * values, axis=1, keepdims=True) + 1e-06)
        blk[OWN, part(t), :] = (values * scale).astype(jnp.bfloat16)

    normalise(0)
    pl.semaphore_wait(barrier, 4)
    send_tags(OWN, A, first).start()
    send_tags(OWN, B, second).start()
    send(OWN, A, 0, first).start()

    def prepare(t, _):
        normalise(t)
        send(OWN, A, t, first).start()
        return 0

    lax.fori_loop(1, chunks, prepare, 0)

    def row(slot, t):
        return tags[slot, pl.ds(t, 1), :]

    def columns(values):
        return jnp.broadcast_to(values, (LANES, LANES)).T

    def fold(values):
        return jnp.max(values.reshape(LANES // 8, 8, LANES), axis=0)

    def scores(p, q_slot, n):
        q = blk[q_slot, 2 * n * LANES:2 * (n + 1) * LANES, :]
        return lax.dot_general(p, q, (((1,), (1,)), ((), ())), preferred_element_type=jnp.float32)

    def own_step(t, _):
        p = blk[OWN, part(t), :]
        labels = columns(row(OWN, chunks + t).astype(jnp.float32))
        down = lax.broadcasted_iota(jnp.int32, (LANES, LANES), 0) + t * LANES
        along = lax.broadcasted_iota(jnp.int32, (LANES, LANES), 1)
        for n in range(chunks // 2):
            s = scores(p, OWN, n)
            for h in range(2):
                tile = 2 * n + h
                ids = row(OWN, tile).astype(jnp.float32)
                hits = (labels == ids) & (down != along + tile * LANES)
                top = fold(jnp.where(hits, s[:, h * LANES:(h + 1) * LANES], OUT))
                at = (0, slice(None), slice(tile * LANES, (tile + 1) * LANES))
                qacc[at] = jnp.maximum(qacc[at], top)
        return 0

    def shared(slot):
        low, high = tags[slot, 0:1, 0:1], tags[slot, chunks - 1:chunks, LANES - 1:LANES]
        if slot == C:
            return low
        return jnp.where(core == (0 if slot == A else 1), low, high)

    def pair_step(p_slot, q_slot, t, cluster, q_at):
        p = blk[p_slot, part(t), :]
        p_bias = columns(jnp.where(row(p_slot, chunks + t) == cluster, 0.0, OUT))
        best = jnp.full((LANES, LANES), OUT, jnp.float32)
        for n in range(chunks // 2):
            s = scores(p, q_slot, n)
            for h in range(2):
                tile = 2 * n + h
                one = s[:, h * LANES:(h + 1) * LANES]
                q_bias = jnp.where(row(q_slot, chunks + tile) == cluster, 0.0, OUT)
                best = jnp.maximum(best, one + q_bias)
                at = (q_at, slice(None), slice(tile * LANES, (tile + 1) * LANES))
                qacc[at] = jnp.maximum(qacc[at], fold(one + p_bias))
        at = (p_slot - 1, slice(None), part(t))
        pres[at] = jnp.maximum(pres[at], fold(best.T))

    lax.fori_loop(0, chunks, own_step, 0)

    c_source = jnp.where(core == 0, A, OWN)
    send_tags(OWN, A, first).wait()
    send_tags(OWN, B, second).wait()
    send_tags(c_source, C, sibling).start()
    send_tags(c_source, C, sibling).wait()
    s_a, s_b, s_c = shared(A), shared(B), shared(C)

    def first_step(t, _):
        send(OWN, A, t, first).wait_recv()
        send(c_source, C, t, sibling).start()
        pair_step(A, OWN, t, s_a, 1)
        send(c_source, C, t, sibling).wait_recv()
        pair_step(C, OWN, t, s_c, 2)
        send(OWN, A, t, first).wait_send()

        @pl.when(t == chunks - 2)
        def _():
            send(OWN, B, 0, second).start()
            send(OWN, B, 1, second).start()

        return 0

    lax.fori_loop(0, chunks, first_step, 0)
    for t in range(2, chunks):
        send(OWN, B, t, second).start()

    def second_step(t, _):
        @pl.when(core == 1)
        def _():
            pair_step(C, A, t, s_c, 4)

        send(OWN, B, t, second).wait_recv()
        pair_step(B, A, t, s_b, 3)

        @pl.when(core == 0)
        def _():
            pair_step(B, C, t, s_b, 4)

        return 0

    lax.fori_loop(0, chunks, second_step, 0)

    def masked(slot, tile, cluster, values):
        lanes = slice(tile * LANES, (tile + 1) * LANES)
        top = jnp.max(values[:, lanes], axis=0, keepdims=True)
        return jnp.where(row(slot, tile) == cluster, top, -1.0)

    def message(which, target):
        return pltpu.make_async_remote_copy(
            src_ref=msg.at[which], dst_ref=got.at[which], send_sem=msg_send.at[which],
            recv_sem=msg_recv.at[which], device_id=target, device_id_type=MESH)

    targets = (second, first, above)
    extra = qacc[4]
    for tile in range(chunks):
        msg[0, tile:tile + 1, :] = jnp.maximum(
            jnp.maximum(masked(A, tile, s_a, pres[0]), masked(A, tile, s_b, qacc[3])),
            jnp.where(core == 1, masked(A, tile, s_c, extra), -1.0))
        msg[1, tile:tile + 1, :] = masked(B, tile, s_b, pres[1])
        msg[2, tile:tile + 1, :] = jnp.maximum(
            masked(C, tile, s_c, pres[2]), jnp.where(core == 0, masked(C, tile, s_b, extra), -1.0))
    for which in range(3):
        message(which, targets[which]).start()
    for tile in range(chunks):
        lanes = slice(tile * LANES, (tile + 1) * LANES)
        own = jnp.max(qacc[0, :, lanes], axis=0, keepdims=True)
        out_ref[tile:tile + 1, :] = jnp.maximum(
            jnp.maximum(own, -1.0),
            jnp.maximum(masked(OWN, tile, s_a, qacc[1]), masked(OWN, tile, s_c, qacc[2])))
    for t in range(chunks):
        send(OWN, B, t, second).wait_send()
        send(c_source, C, t, sibling).wait_send()
    for which in range(3):
        message(which, targets[which]).wait()
    out_ref[...] = jnp.maximum(jnp.maximum(out_ref[...], got[0]), jnp.maximum(got[1], got[2]))


def shards(n_slab, n_member, embeddings, cluster_ids, keep_mask):
    rows, width = embeddings.shape
    chunks = rows // LANES
    vmem = pl.BlockSpec(memory_space=pltpu.VMEM)
    highest = pl.pallas_call(
        functools.partial(kernel, n_slab, n_member),
        out_shape=jax.ShapeDtypeStruct((chunks, LANES), jnp.float32),
        in_specs=[pl.BlockSpec(memory_space=pltpu.HBM), vmem, vmem],
        out_specs=vmem,
        scratch_shapes=[
            pltpu.VMEM((rows, width), jnp.bfloat16),
            pltpu.VMEM((4, rows, width), jnp.bfloat16),
            pltpu.VMEM((4, 2 * chunks, LANES), jnp.int32),
            pltpu.VMEM((3, 8, rows), jnp.float32),
            pltpu.VMEM((5, 8, rows), jnp.float32),
            pltpu.VMEM((3, chunks, LANES), jnp.float32),
            pltpu.VMEM((3, chunks, LANES), jnp.float32),
            pltpu.SemaphoreType.DMA((chunks,)),
            pltpu.SemaphoreType.DMA((4, chunks)),
            pltpu.SemaphoreType.DMA((4, chunks)),
            pltpu.SemaphoreType.DMA((4,)),
            pltpu.SemaphoreType.DMA((4,)),
            pltpu.SemaphoreType.DMA((3,)),
            pltpu.SemaphoreType.DMA((3,)),
        ],
        compiler_params=pltpu.CompilerParams(
            collective_id=0, has_side_effects=True, vmem_limit_bytes=40 << 20),
    )(embeddings, cluster_ids.reshape(chunks, LANES), keep_mask.reshape(chunks, LANES))
    return highest.reshape(rows)


def solution(mesh):
    placed = (P(("slab", "member"), None), P(("slab", "member")), P(("slab", "member")))
    return jax.shard_map(
        functools.partial(shards, mesh.shape["slab"], mesh.shape["member"]),
        mesh=mesh, in_specs=placed, out_specs=P(("slab", "member")), check_vma=False,
    )
```

time: 244 us -> 61.3 us (0.25)
  the two profiles are of different devices: /device:TPU:4 before, /device:TPU:1 now
where the time goes in v1:
time: 61.3 us; the launch traced here: 61.1 us
  Pallas kernels  57.7 us (94%)
  local copies, waits for them, and re-layouts  3.38 us (6%)
    pallas_call x1, Pallas kernels, shards(): pl.pallas_call(functools.partial(kernel, n_slab, n_member), out_shape=jax...  57.7 us
    unnamed x7, local copies, waits for them, and re-layouts  3.38 us

profile of v1, /device:TPU:1, one launch (start us, length us, event | category | flops | bytes accessed | tf_op | source)
XLA Modules:
  0.0 61.1 jit_solution(15219938620042629236)
XLA Ops:
  0.0 0.0 copy-start
  0.0 1.4 %copy-done = bf16[1024,768]{1,0:T(8,128)(2,1)S(1)} copy-done((bf16[1024,768]{1,0:T(8,128)(2,1)S(1)}, bf16[1024,768]{1,0:T(8,128)(2,1)}, u32[]{:S(2)}) %copy-start) | copy-done | bytes 1572888
  1.4 0.0 copy-start.1
  1.4 0.7 %copy-done.1 = s32[1024]{0:T(1024)S(1)} copy-done((s32[1024]{0:T(1024)S(1)}, s32[1024]{0:T(1024)}, u32[]{:S(2)}) %copy-start.1) | copy-done | bytes 4120
  2.1 0.0 copy-start.2
  2.1 0.7 %copy-done.2 = s32[1024]{0:T(1024)S(1)} copy-done((s32[1024]{0:T(1024)S(1)}, s32[1024]{0:T(1024)}, u32[]{:S(2)}) %copy-start.2) | copy-done | bytes 4120
  2.8 57.7 %shard_map.37 = f32[8,128]{1,0:T(8,128)S(1)} custom-call(bf16[1024,768]{1,0:T(8,128)(2,1)S(1)} %copy-done, s32[8,128]{1,0:T(8,128)S(1)} %bitcast.4, s32[8,128]{1,0:T(8,128)S(1)} %bitcast.5), custom_call_target="tpu_custom_call" | custom-call | tf_op jit(solution)/shard_map/pallas_call | solution.py:215
  60.5 0.6 copy.5
Async XLA Ops:
  0.0 1.4 %copy-start = (bf16[1024,768]{1,0:T(8,128)(2,1)S(1)}, bf16[1024,768]{1,0:T(8,128)(2,1)}, u32[]{:S(2)}) copy-start(bf16[1024,768]{1,0:T(8,128)(2,1)} %x_ref.1) | copy-start | bytes 4718596
  1.4 0.7 %copy-start.1 = (s32[1024]{0:T(1024)S(1)}, s32[1024]{0:T(1024)}, u32[]{:S(2)}) copy-start(s32[1024]{0:T(1024)} %param.4) | copy-start | bytes 12292
  2.1 0.7 %copy-start.2 = (s32[1024]{0:T(1024)S(1)}, s32[1024]{0:T(1024)}, u32[]{:S(2)}) copy-start(s32[1024]{0:T(1024)} %param.5) | copy-start | bytes 12292

commit v2 on v1

v2 whole, which is shorter than its diff:
```python
import functools

import jax
import jax.numpy as jnp
from jax import lax
from jax.experimental import pallas as pl
from jax.experimental.pallas import tpu as pltpu
from jax.sharding import PartitionSpec as P

MESH = pl.DeviceIdType.MESH
OWN, A, B, C = 0, 1, 2, 3
LANES = 128
OUT = -4.0


def kernel(n_slab, n_member, x_ref, ids_ref, keep_ref, out_ref, raw, blk, tags, pres, qacc, msg, got,
           load_sem, send_sem, recv_sem, tag_send, tag_recv, msg_send, msg_recv):
    rows, width = raw.shape
    chunks = rows // LANES
    count = n_slab * n_member
    slab, member = lax.axis_index("slab"), lax.axis_index("member")
    core = lax.rem(member, 2)
    place = slab * n_member + member
    chip = lax.div(place, 2)
    has_down, has_up = chip > 0, chip < count // 2 - 1
    even, odd = core == 0, core == 1

    def device(at):
        at = jnp.clip(at, 0, count - 1)
        return (lax.div(at, n_member), lax.rem(at, n_member))

    first, second = device(place - 2 + 4 * core), device(place + 2 - 4 * core)
    has_first = (even & has_down) | (odd & has_up)
    has_second = (even & has_up) | (odd & has_down)
    has_a, has_b, has_c = has_second, has_first, even | has_up
    gives_c = odd | has_up
    c_source = jnp.where(even, A, OWN)
    sibling = (slab, member + 1 - 2 * core)
    above, below = device(place + 1), device(place - 1)

    barrier = pltpu.get_barrier_semaphore()
    partners = ((has_first, first), (has_second, second), (place < count - 1, above), (place > 0, below))
    for there, other in partners:
        @pl.when(there)
        def _():
            pl.semaphore_signal(barrier, inc=1, device_id=other, device_id_type=MESH)

    def part(t):
        return pl.ds(pl.multiple_of(t * LANES, LANES), LANES)

    def pair_of_parts(t):
        return pl.ds(pl.multiple_of(t * 2 * LANES, 2 * LANES), 2 * LANES)

    def load(t):
        return pltpu.make_async_copy(x_ref.at[part(t)], raw.at[part(t)], load_sem.at[t])

    def send(src_slot, dst_slot, t, target):
        return pltpu.make_async_remote_copy(
            src_ref=blk.at[src_slot, part(t)], dst_ref=blk.at[dst_slot, part(t)],
            send_sem=send_sem.at[dst_slot, t], recv_sem=recv_sem.at[dst_slot, t],
            device_id=target, device_id_type=MESH)

    def send_tags(src_slot, dst_slot, target):
        return pltpu.make_async_remote_copy(
            src_ref=tags.at[src_slot], dst_ref=tags.at[dst_slot], send_sem=tag_send.at[dst_slot],
            recv_sem=tag_recv.at[dst_slot], device_id=target, device_id_type=MESH)

    load_ids = pltpu.make_async_copy(ids_ref, tags.at[OWN, 0:chunks], load_sem.at[chunks])
    load_keep = pltpu.make_async_copy(keep_ref, tags.at[OWN, chunks:2 * chunks], load_sem.at[chunks + 1])
    load(0).start()
    load_ids.start()
    load_keep.start()
    for t in range(1, chunks):
        load(t).start()
    for slot, there in ((A, has_a), (B, has_b), (C, has_c)):
        @pl.when(jnp.logical_not(there))
        def _():
            tags[slot] = jnp.full(tags.shape[1:], -2, jnp.int32)
    pres[...] = jnp.full(pres.shape, OUT, jnp.float32)
    qacc[...] = jnp.full(qacc.shape, OUT, jnp.float32)

    def normalise(t):
        load(t).wait()
        values = raw[part(t), :].astype(jnp.float32)
        scale = lax.rsqrt(jnp.sum(values * values, axis=1, keepdims=True) + 1e-06)
        blk[OWN, part(t), :] = (values * scale).astype(jnp.bfloat16)

    normalise(0)
    load_ids.wait()
    load_keep.wait()
    tags[OWN, chunks:2 * chunks] = jnp.where(tags[OWN, chunks:2 * chunks] == 1, tags[OWN, 0:chunks], -1)
    pl.semaphore_wait(barrier, sum(there.astype(jnp.int32) for there, _ in partners))

    @pl.when(has_first)
    def _():
        send(OWN, A, 0, first).start()
        send_tags(OWN, A, first).start()

    @pl.when(has_second)
    def _():
        send_tags(OWN, B, second).start()

    def prepare(t, _):
        normalise(t)

        @pl.when(has_first)
        def _():
            send(OWN, A, t, first).start()

        return 0

    lax.fori_loop(1, chunks, prepare, 0)

    def row(slot, t):
        return tags[slot, pl.ds(t, 1), :]

    def columns(values):
        return jnp.broadcast_to(values, (LANES, LANES)).T

    def fold(values):
        return jnp.max(values.reshape(values.shape[0] // 8, 8, LANES), axis=0)

    def scores(p, q_slot, n):
        q = blk[q_slot, 2 * n * LANES:2 * (n + 1) * LANES, :]
        return lax.dot_general(p, q, (((1,), (1,)), ((), ())), preferred_element_type=jnp.float32)

    def own_step(t, _):
        p = blk[OWN, pair_of_parts(t), :]
        labels = jnp.concatenate(
            [columns(row(OWN, chunks + 2 * t + i).astype(jnp.float32)) for i in range(2)], axis=0)
        down = lax.broadcasted_iota(jnp.int32, (2 * LANES, LANES), 0) + t * 2 * LANES
        along = lax.broadcasted_iota(jnp.int32, (2 * LANES, LANES), 1)
        for n in range(chunks // 2):
            s = scores(p, OWN, n)
            for h in range(2):
                tile = 2 * n + h
                ids = row(OWN, tile).astype(jnp.float32)
                hits = (labels == ids) & (down != along + tile * LANES)
                top = fold(jnp.where(hits, s[:, h * LANES:(h + 1) * LANES], OUT))
                at = (0, slice(None), slice(tile * LANES, (tile + 1) * LANES))
                qacc[at] = jnp.maximum(qacc[at], top)
        return 0

    def shared(slot):
        low, high = tags[slot, 0:1, 0:1], tags[slot, chunks - 1:chunks, LANES - 1:LANES]
        if slot == C:
            return low
        return jnp.where(core == (0 if slot == A else 1), low, high)

    def pair_step(p_slot, q_slot, t, size, cluster, q_at):
        p = blk[p_slot, pair_of_parts(t) if size == 2 else part(t), :]
        p_bias = [columns(jnp.where(row(p_slot, chunks + size * t + i) == cluster, 0.0, OUT)) for i in range(size)]
        p_bias = jnp.concatenate(p_bias, axis=0) if size > 1 else p_bias[0]
        best = jnp.full((size * LANES, LANES), OUT, jnp.float32)
        for n in range(chunks // 2):
            s = scores(p, q_slot, n)
            for h in range(2):
                tile = 2 * n + h
                one = s[:, h * LANES:(h + 1) * LANES]
                q_bias = jnp.where(row(q_slot, chunks + tile) == cluster, 0.0, OUT)
                best = jnp.maximum(best, one + q_bias)
                at = (q_at, slice(None), slice(tile * LANES, (tile + 1) * LANES))
                qacc[at] = jnp.maximum(qacc[at], fold(one + p_bias))
        for i in range(size):
            at = (p_slot - 1, slice(None), part(size * t + i))
            pres[at] = jnp.maximum(pres[at], fold(best[i * LANES:(i + 1) * LANES].T))

    lax.fori_loop(0, chunks // 2, own_step, 0)

    @pl.when(has_first)
    def _():
        send_tags(OWN, A, first).wait_send()

    @pl.when(has_second)
    def _():
        send_tags(OWN, B, second).wait_send()

    @pl.when(has_a)
    def _():
        send_tags(OWN, A, first).wait_recv()

    @pl.when(has_b)
    def _():
        send_tags(OWN, B, second).wait_recv()

    @pl.when(gives_c)
    def _():
        send_tags(c_source, C, sibling).start()
        send_tags(c_source, C, sibling).wait_send()

    @pl.when(has_c)
    def _():
        send_tags(c_source, C, sibling).wait_recv()

    s_a, s_b, s_c = shared(A), shared(B), shared(C)
    early = 2

    def first_step(t, _):
        @pl.when((t == chunks // 2 - 1) & has_first)
        def _():
            for i in range(chunks - 2):
                send(OWN, A, i, first).wait_send()

        @pl.when((t == chunks // 2 - 1) & has_second)
        def _():
            for i in range(early):
                send(OWN, B, i, second).start()

        for i in range(2):
            @pl.when(has_a)
            def _():
                send(OWN, A, 2 * t + i, first).wait_recv()

            @pl.when(gives_c)
            def _():
                send(c_source, C, 2 * t + i, sibling).start()

        @pl.when((t == chunks // 2 - 1) & has_second)
        def _():
            for i in range(early, chunks):
                send(OWN, B, i, second).start()

        @pl.when(has_a)
        def _():
            pair_step(A, OWN, t, 2, s_a, 1)

        @pl.when(has_c)
        def _():
            for i in range(2):
                send(c_source, C, 2 * t + i, sibling).wait_recv()
            pair_step(C, OWN, t, 2, s_c, 2)

        return 0

    lax.fori_loop(0, chunks // 2, first_step, 0)

    @pl.when(odd & has_a & has_c)
    def _():
        def extra_step(t, _):
            pair_step(C, A, t, 2, s_c, 4)
            return 0

        lax.fori_loop(0, chunks // 2, extra_step, 0)

    def second_step(t, _):
        @pl.when(has_b)
        def _():
            send(OWN, B, t, second).wait_recv()

        @pl.when(has_a & has_b)
        def _():
            pair_step(B, A, t, 1, s_b, 3)

        @pl.when(even & has_b)
        def _():
            pair_step(B, C, t, 1, s_b, 4)

        return 0

    lax.fori_loop(0, chunks, second_step, 0)

    def masked(slot, tile, cluster, values):
        lanes = slice(tile * LANES, (tile + 1) * LANES)
        top = jnp.max(values[:, lanes], axis=0, keepdims=True)
        return jnp.where(row(slot, tile) == cluster, top, -1.0)

    def message(which, target):
        return pltpu.make_async_remote_copy(
            src_ref=msg.at[which], dst_ref=got.at[which], send_sem=msg_send.at[which],
            recv_sem=msg_recv.at[which], device_id=target, device_id_type=MESH)

    messages = ((has_a, second, has_first), (has_b, first, has_second), (has_c, above, odd | has_down))
    extra = qacc[4]
    for tile in range(chunks):
        msg[0, tile:tile + 1, :] = jnp.maximum(
            jnp.maximum(masked(A, tile, s_a, pres[0]), masked(A, tile, s_b, qacc[3])),
            jnp.where(odd, masked(A, tile, s_c, extra), -1.0))
        msg[1, tile:tile + 1, :] = masked(B, tile, s_b, pres[1])
        msg[2, tile:tile + 1, :] = jnp.maximum(
            masked(C, tile, s_c, pres[2]), jnp.where(even, masked(C, tile, s_b, extra), -1.0))
    for which, (gives, target, _) in enumerate(messages):
        @pl.when(gives)
        def _():
            message(which, target).start()
    for tile in range(chunks):
        lanes = slice(tile * LANES, (tile + 1) * LANES)
        own = jnp.max(qacc[0, :, lanes], axis=0, keepdims=True)
        out_ref[tile:tile + 1, :] = jnp.maximum(
            jnp.maximum(own, -1.0),
            jnp.maximum(masked(OWN, tile, s_a, qacc[1]), masked(OWN, tile, s_c, qacc[2])))

    @pl.when(has_first)
    def _():
        for t in range(chunks - 2, chunks):
            send(OWN, A, t, first).wait_send()

    @pl.when(has_second)
    def _():
        for t in range(chunks):
            send(OWN, B, t, second).wait_send()

    @pl.when(gives_c)
    def _():
        for t in range(chunks):
            send(c_source, C, t, sibling).wait_send()

    for which, (gives, target, gets) in enumerate(messages):
        @pl.when(gives)
        def _():
            message(which, target).wait_send()

        @pl.when(gets)
        def _():
            message(which, target).wait_recv()
            out_ref[...] = jnp.maximum(out_ref[...], got[which])


def shards(n_slab, n_member, embeddings, cluster_ids, keep_mask):
    rows, width = embeddings.shape
    chunks = rows // LANES
    highest = pl.pallas_call(
        functools.partial(kernel, n_slab, n_member),
        out_shape=jax.ShapeDtypeStruct((chunks, LANES), jnp.float32),
        in_specs=[pl.BlockSpec(memory_space=pltpu.HBM)] * 3,
        out_specs=pl.BlockSpec(memory_space=pltpu.VMEM),
        scratch_shapes=[
            pltpu.VMEM((rows, width), jnp.bfloat16),
            pltpu.VMEM((4, rows, width), jnp.bfloat16),
            pltpu.VMEM((4, 2 * chunks, LANES), jnp.int32),
            pltpu.VMEM((3, 8, rows), jnp.float32),
            pltpu.VMEM((5, 8, rows), jnp.float32),
            pltpu.VMEM((3, chunks, LANES), jnp.float32),
            pltpu.VMEM((3, chunks, LANES), jnp.float32),
            pltpu.SemaphoreType.DMA((chunks + 2,)),
            pltpu.SemaphoreType.DMA((4, chunks)),
            pltpu.SemaphoreType.DMA((4, chunks)),
            pltpu.SemaphoreType.DMA((4,)),
            pltpu.SemaphoreType.DMA((4,)),
            pltpu.SemaphoreType.DMA((3,)),
            pltpu.SemaphoreType.DMA((3,)),
        ],
        compiler_params=pltpu.CompilerParams(
            collective_id=0, has_side_effects=True, vmem_limit_bytes=60 << 20),
    )(embeddings, cluster_ids.reshape(chunks, LANES), keep_mask.reshape(chunks, LANES))
    return highest.reshape(rows)


def solution(mesh):
    placed = (P(("slab", "member"), None), P(("slab", "member")), P(("slab", "member")))
    return jax.shard_map(
        functools.partial(shards, mesh.shape["slab"], mesh.shape["member"]),
        mesh=mesh, in_specs=placed, out_specs=P(("slab", "member")), check_vma=False,
    )
```

time: 61.3 us -> 53.8 us (0.88)
  the two profiles are of different devices: /device:TPU:1 before, /device:TPU:7 now
where the time goes in v2:
time: 53.8 us; the launch traced here: 53 us
  Pallas kernels  51.7 us (96%)
  local copies, waits for them, and re-layouts  1.28 us (2%)
    pallas_call x1, Pallas kernels, shards(): pl.pallas_call(functools.partial(kernel, n_slab, n_member), out_shape=jax...  51.7 us
    unnamed x1, local copies, waits for them, and re-layouts  1.28 us

profile of v2, /device:TPU:7, one launch (start us, length us, event | category | flops | bytes accessed | tf_op | source)
XLA Modules:
  0.0 53.0 jit_solution(13859801736479920384)
XLA Ops:
  0.0 51.7 %shard_map.37 = f32[8,128]{1,0:T(8,128)} custom-call(bf16[1024,768]{1,0:T(8,128)(2,1)} %x_ref.1, s32[8,128]{1,0:T(8,128)} %bitcast.4, s32[8,128]{1,0:T(8,128)} %bitcast.5), custom_call_target="tpu_custom_call" | custom-call | tf_op jit(solution)/shard_map/pallas_call | solution.py:321
  51.7 1.3 %copy.5 = f32[1024]{0:T(1024)} copy(f32[1024]{0:T(1024)} %bitcast.3) | data formatting | bytes 8192

commit v3 on v2

v3 whole, which is shorter than its diff:
```python
import functools

import jax
import jax.numpy as jnp
from jax import lax
from jax.experimental import pallas as pl
from jax.experimental.pallas import tpu as pltpu
from jax.sharding import PartitionSpec as P

MESH = pl.DeviceIdType.MESH
OWN, A, B, C = 0, 1, 2, 3
LANES = 128
GROUP = 2 * LANES
LEAD = 4
OUT = -4.0


def kernel(n_slab, n_member, x_ref, ids_ref, keep_ref, out_ref, raw, blk, tags, pres, qacc, msg, got,
           load_sem, send_sem, recv_sem, tag_send, tag_recv, msg_send, msg_recv):
    rows, width = raw.shape
    chunks, groups = rows // LANES, rows // GROUP
    count = n_slab * n_member
    slab, member = lax.axis_index("slab"), lax.axis_index("member")
    core = lax.rem(member, 2)
    place = slab * n_member + member
    chip = lax.div(place, 2)
    has_down, has_up = chip > 0, chip < count // 2 - 1
    even, odd = core == 0, core == 1

    def device(at):
        at = jnp.clip(at, 0, count - 1)
        return (lax.div(at, n_member), lax.rem(at, n_member))

    first, second = device(place - 2 + 4 * core), device(place + 2 - 4 * core)
    has_first = (even & has_down) | (odd & has_up)
    has_second = (even & has_up) | (odd & has_down)
    has_a, has_b, has_c = has_second, has_first, even | has_up
    gives_c = odd | has_up
    c_source = jnp.where(even, A, OWN)
    sibling = (slab, member + 1 - 2 * core)
    above, below = device(place + 1), device(place - 1)

    barrier = pltpu.get_barrier_semaphore()
    partners = ((has_first, first), (has_second, second), (place < count - 1, above), (place > 0, below))
    for there, other in partners:
        @pl.when(there)
        def _():
            pl.semaphore_signal(barrier, inc=1, device_id=other, device_id_type=MESH)

    def part(t):
        return pl.ds(pl.multiple_of(t * LANES, LANES), LANES)

    def group_at(g):
        return pl.ds(pl.multiple_of(g * GROUP, GROUP), GROUP)

    def order(slot, t, count):
        if slot == C:
            return t
        flip = core if slot == A else 1 - core
        return t + flip * (count - 1 - 2 * t)

    def load(t):
        return pltpu.make_async_copy(x_ref.at[part(t)], raw.at[part(t)], load_sem.at[t])

    def send(slot, t):
        source, target = {A: (OWN, first), B: (OWN, second), C: (c_source, sibling)}[slot]
        rows_of = part(order(slot, t, chunks))
        return pltpu.make_async_remote_copy(
            src_ref=blk.at[source, rows_of], dst_ref=blk.at[slot, rows_of],
            send_sem=send_sem.at[slot, t], recv_sem=recv_sem.at[slot, t],
            device_id=target, device_id_type=MESH)

    def send_tags(src_slot, dst_slot, target):
        return pltpu.make_async_remote_copy(
            src_ref=tags.at[src_slot], dst_ref=tags.at[dst_slot], send_sem=tag_send.at[dst_slot],
            recv_sem=tag_recv.at[dst_slot], device_id=target, device_id_type=MESH)

    load_ids = pltpu.make_async_copy(ids_ref, tags.at[OWN, 0:chunks], load_sem.at[chunks])
    load_keep = pltpu.make_async_copy(keep_ref, tags.at[OWN, chunks:2 * chunks], load_sem.at[chunks + 1])
    load(order(A, 0, chunks)).start()
    load_ids.start()
    load_keep.start()
    for t in range(1, chunks):
        load(order(A, t, chunks)).start()
    for slot, there in ((A, has_a), (B, has_b), (C, has_c)):
        @pl.when(jnp.logical_not(there))
        def _():
            tags[slot] = jnp.full(tags.shape[1:], -2, jnp.int32)
    pres[...] = jnp.full(pres.shape, OUT, jnp.float32)
    qacc[...] = jnp.full(qacc.shape, OUT, jnp.float32)

    def normalise(t):
        load(t).wait()
        values = raw[part(t), :].astype(jnp.float32)
        scale = lax.rsqrt(jnp.sum(values * values, axis=1, keepdims=True) + 1e-06)
        blk[OWN, part(t), :] = (values * scale).astype(jnp.bfloat16)

    normalise(order(A, 0, chunks))
    load_ids.wait()
    load_keep.wait()
    tags[OWN, chunks:2 * chunks] = jnp.where(tags[OWN, chunks:2 * chunks] == 1, tags[OWN, 0:chunks], -1)
    pl.semaphore_wait(barrier, sum(there.astype(jnp.int32) for there, _ in partners))

    @pl.when(has_first)
    def _():
        send(A, 0).start()
        send_tags(OWN, A, first).start()

    @pl.when(has_second)
    def _():
        send_tags(OWN, B, second).start()

    def prepare(t, _):
        normalise(order(A, t, chunks))

        @pl.when(has_first)
        def _():
            send(A, t).start()

        return 0

    lax.fori_loop(1, chunks, prepare, 0)

    @pl.when(odd)
    def _():
        for t in range(chunks):
            send(C, t).start()

    def row(slot, t):
        return tags[slot, pl.ds(t, 1), :]

    def columns(values):
        return jnp.broadcast_to(values, (LANES, LANES)).T

    def fold(values):
        return jnp.max(values.reshape(values.shape[0] // 8, 8, LANES), axis=0)

    def scores(p, q_slot, g):
        q = blk[q_slot, group_at(g), :]
        return lax.dot_general(p, q, (((1,), (1,)), ((), ())), preferred_element_type=jnp.float32)

    def own_step(t, _):
        p = blk[OWN, group_at(t), :]
        labels = jnp.concatenate(
            [columns(row(OWN, chunks + 2 * t + i).astype(jnp.float32)) for i in range(2)], axis=0)
        down = lax.broadcasted_iota(jnp.int32, (2 * LANES, LANES), 0) + t * 2 * LANES
        along = lax.broadcasted_iota(jnp.int32, (2 * LANES, LANES), 1)
        for n in range(chunks // 2):
            s = scores(p, OWN, n)
            for h in range(2):
                tile = 2 * n + h
                ids = row(OWN, tile).astype(jnp.float32)
                hits = (labels == ids) & (down != along + tile * LANES)
                top = fold(jnp.where(hits, s[:, h * LANES:(h + 1) * LANES], OUT))
                at = (0, slice(None), slice(tile * LANES, (tile + 1) * LANES))
                qacc[at] = jnp.maximum(qacc[at], top)
        return 0

    def shared(slot):
        low, high = tags[slot, 0:1, 0:1], tags[slot, chunks - 1:chunks, LANES - 1:LANES]
        if slot == C:
            return low
        return jnp.where(core == (0 if slot == A else 1), low, high)

    def biases(p_slot, t, size, cluster):
        each = [columns(jnp.where(row(p_slot, chunks + t + i) == cluster, 0.0, OUT)) for i in range(size)]
        return jnp.concatenate(each, axis=0) if size > 1 else each[0]

    def tile_pair(p, p_bias, best, q_slot, g, cluster, q_at):
        s = scores(p, q_slot, g)
        for h in range(2):
            one = s[:, h * LANES:(h + 1) * LANES]
            q_bias = jnp.where(row(q_slot, chunks + 2 * g + h) == cluster, 0.0, OUT)
            best = jnp.maximum(best, one + q_bias)
            at = (q_at, slice(None), part(2 * g + h))
            qacc[at] = jnp.maximum(qacc[at], fold(one + p_bias))
        return best

    def keep_rows(p_slot, t, size, best):
        for i in range(size):
            at = (p_slot - 1, slice(None), part(t + i))
            pres[at] = jnp.maximum(pres[at], fold(best[i * LANES:(i + 1) * LANES].T))

    def whole(p_slot, t, size, q_slot, cluster, q_at):
        p = blk[p_slot, pl.ds(pl.multiple_of(t * LANES, LANES), size * LANES), :]
        p_bias = biases(p_slot, t, size, cluster)
        best = jnp.full((size * LANES, LANES), OUT, jnp.float32)
        for g in range(groups):
            best = tile_pair(p, p_bias, best, q_slot, g, cluster, q_at)
        keep_rows(p_slot, t, size, best)

    def some(p_slot, g, q_slot, arrivals, cluster, q_at):
        p = blk[p_slot, group_at(g), :]
        p_bias = biases(p_slot, 2 * g, 2, cluster)
        best = jnp.full((GROUP, LANES), OUT, jnp.float32)
        for i in arrivals:
            best = tile_pair(p, p_bias, best, q_slot, order(q_slot, i, groups), cluster, q_at)
        keep_rows(p_slot, 2 * g, 2, best)

    lax.fori_loop(0, groups, own_step, 0)

    @pl.when(has_first)
    def _():
        for t in range(LEAD):
            send(A, t).wait_send()

    @pl.when(has_second)
    def _():
        for t in range(chunks):
            send(B, t).start()

    @pl.when(has_first)
    def _():
        send_tags(OWN, A, first).wait_send()

    @pl.when(has_second)
    def _():
        send_tags(OWN, B, second).wait_send()

    @pl.when(has_a)
    def _():
        send_tags(OWN, A, first).wait_recv()

    @pl.when(has_b)
    def _():
        send_tags(OWN, B, second).wait_recv()

    @pl.when(gives_c)
    def _():
        send_tags(c_source, C, sibling).start()
        send_tags(c_source, C, sibling).wait_send()

    @pl.when(has_c)
    def _():
        send_tags(c_source, C, sibling).wait_recv()

    s_a, s_b, s_c = shared(A), shared(B), shared(C)

    @pl.when(even)
    def _():
        for t in range(chunks):
            send(C, t).wait_recv()

    def step(j, _):
        @pl.when(has_a)
        def _():
            send(A, 2 * j).wait_recv()
            send(A, 2 * j + 1).wait_recv()

        @pl.when(even & has_a)
        def _():
            send(C, 2 * j).start()
            send(C, 2 * j + 1).start()

        @pl.when(has_a)
        def _():
            whole(A, 2 * order(A, j, groups), 2, OWN, s_a, 1)

        @pl.when(odd & has_c)
        def _():
            send(C, 2 * j).wait_recv()
            send(C, 2 * j + 1).wait_recv()

        @pl.when(has_c)
        def _():
            whole(C, 2 * j, 2, OWN, s_c, 2)

        for now in range(groups):
            @pl.when(odd & has_a & has_c & (j == now))
            def _():
                some(C, now, A, range(now + 1), s_c, 4)
                if now > 0:
                    some(A, order(A, now, groups), C, range(now), s_a, 5)

        m = j - 1

        @pl.when(has_b & (j > 0))
        def _():
            send(B, 2 * m).wait_recv()
            send(B, 2 * m + 1).wait_recv()

            @pl.when(even)
            def _():
                whole(B, 2 * order(B, m, groups), 2, C, s_b, 4)

            for now in range(groups - 1):
                @pl.when(has_a & (m == now))
                def _():
                    some(B, order(B, now, groups), A, range(min(now + 2, groups - now)), s_b, 3)

        return 0

    lax.fori_loop(0, groups, step, 0)

    def message(which, target):
        return pltpu.make_async_remote_copy(
            src_ref=msg.at[which], dst_ref=got.at[which], send_sem=msg_send.at[which],
            recv_sem=msg_recv.at[which], device_id=target, device_id_type=MESH)

    def masked(slot, tile, cluster, values):
        lanes = slice(tile * LANES, (tile + 1) * LANES)
        best = jnp.max(values[:, lanes], axis=0, keepdims=True)
        return jnp.where(row(slot, tile) == cluster, best, -1.0)

    @pl.when(odd & has_c)
    def _():
        for tile in range(chunks):
            msg[2, tile:tile + 1, :] = jnp.maximum(masked(C, tile, s_c, pres[2]), masked(C, tile, s_a, qacc[5]))
        message(2, above).start()

    @pl.when(has_a & has_b)
    def _():
        some(B, order(B, 0, groups), A, range(2, groups), s_b, 3)

    def last_step(t, _):
        @pl.when(has_b)
        def _():
            send(B, t).wait_recv()

        @pl.when(even & has_b)
        def _():
            whole(B, order(B, t, chunks), 1, C, s_b, 4)

        return 0

    lax.fori_loop(chunks - 2, chunks, last_step, 0)

    @pl.when(has_a & has_b)
    def _():
        some(B, order(B, groups - 1, groups), A, range(1), s_b, 3)

    for tile in range(chunks):
        msg[0, tile:tile + 1, :] = jnp.maximum(
            jnp.maximum(masked(A, tile, s_a, pres[0]), masked(A, tile, s_b, qacc[3])),
            jnp.where(odd, masked(A, tile, s_c, qacc[4]), -1.0))
        msg[1, tile:tile + 1, :] = masked(B, tile, s_b, pres[1])

    @pl.when(has_a)
    def _():
        message(0, second).start()

    @pl.when(has_b)
    def _():
        message(1, first).start()

    @pl.when(even)
    def _():
        for tile in range(chunks):
            msg[2, tile:tile + 1, :] = jnp.maximum(masked(C, tile, s_c, pres[2]), masked(C, tile, s_b, qacc[4]))
        message(2, above).start()

    messages = ((has_a, second, has_first), (has_b, first, has_second), (has_c, above, odd | has_down))
    for tile in range(chunks):
        lanes = slice(tile * LANES, (tile + 1) * LANES)
        own = jnp.max(qacc[0, :, lanes], axis=0, keepdims=True)
        out_ref[tile:tile + 1, :] = jnp.maximum(
            jnp.maximum(own, -1.0),
            jnp.maximum(masked(OWN, tile, s_a, qacc[1]), masked(OWN, tile, s_c, qacc[2])))

    @pl.when(has_first)
    def _():
        for t in range(LEAD, chunks):
            send(A, t).wait_send()

    @pl.when(has_second)
    def _():
        for t in range(chunks):
            send(B, t).wait_send()

    @pl.when(gives_c)
    def _():
        for t in range(chunks):
            send(C, t).wait_send()

    for which, (gives, target, gets) in enumerate(messages):
        @pl.when(gives)
        def _():
            message(which, target).wait_send()

        @pl.when(gets)
        def _():
            message(which, target).wait_recv()
            out_ref[...] = jnp.maximum(out_ref[...], got[which])


def shards(n_slab, n_member, embeddings, cluster_ids, keep_mask):
    rows, width = embeddings.shape
    chunks = rows // LANES
    highest = pl.pallas_call(
        functools.partial(kernel, n_slab, n_member),
        out_shape=jax.ShapeDtypeStruct((chunks, LANES), jnp.float32),
        in_specs=[pl.BlockSpec(memory_space=pltpu.HBM)] * 3,
        out_specs=pl.BlockSpec(memory_space=pltpu.VMEM),
        scratch_shapes=[
            pltpu.VMEM((rows, width), jnp.bfloat16),
            pltpu.VMEM((4, rows, width), jnp.bfloat16),
            pltpu.VMEM((4, 2 * chunks, LANES), jnp.int32),
            pltpu.VMEM((3, 8, rows), jnp.float32),
            pltpu.VMEM((6, 8, rows), jnp.float32),
            pltpu.VMEM((3, chunks, LANES), jnp.float32),
            pltpu.VMEM((3, chunks, LANES), jnp.float32),
            pltpu.SemaphoreType.DMA((chunks + 2,)),
            pltpu.SemaphoreType.DMA((4, chunks)),
            pltpu.SemaphoreType.DMA((4, chunks)),
            pltpu.SemaphoreType.DMA((4,)),
            pltpu.SemaphoreType.DMA((4,)),
            pltpu.SemaphoreType.DMA((3,)),
            pltpu.SemaphoreType.DMA((3,)),
        ],
        compiler_params=pltpu.CompilerParams(
            collective_id=0, has_side_effects=True, vmem_limit_bytes=40 << 20),
    )(*(pltpu.with_memory_space_constraint(each, pltpu.HBM) for each in (
        embeddings, cluster_ids.reshape(chunks, LANES), keep_mask.reshape(chunks, LANES))))
    return highest.reshape(rows)


def solution(mesh):
    placed = (P(("slab", "member"), None), P(("slab", "member")), P(("slab", "member")))
    return jax.shard_map(
        functools.partial(shards, mesh.shape["slab"], mesh.shape["member"]),
        mesh=mesh, in_specs=placed, out_specs=P(("slab", "member")), check_vma=False,
    )
```

time: 53.8 us -> 51 us (0.948); the launches traced: 53 us -> 50.9 us
  Pallas kernels: 51.7 us -> 50.3 us
  local copies, waits for them, and re-layouts: 1.28 us -> 0.6 us
    pallas_call x1, Pallas kernels: 51.7 us -> 50.3 us  [shards(): pl.pallas_call(functools.partial(kernel, n_slab, n_member), out_shape=jax...]
    unnamed x1, local copies, waits for them, and re-layouts: 1.28 us -> 0.6 us
where the time goes in v3:
time: 51 us; the launch traced here: 50.9 us
  Pallas kernels  50.3 us (99%)
  local copies, waits for them, and re-layouts  0.6 us (1%)
    pallas_call x1, Pallas kernels, shards(): pl.pallas_call(functools.partial(kernel, n_slab, n_member), out_shape=jax...  50.3 us

profile of v3, /device:TPU:7, one launch (start us, length us, event | category | flops | bytes accessed | tf_op | source)
XLA Modules:
  0.0 50.9 jit_solution(9160681171630588906)
XLA Ops:
  0.0 50.3 %shard_map.37 = f32[8,128]{1,0:T(8,128)S(1)} custom-call(bf16[1024,768]{1,0:T(8,128)(2,1)} %x_ref.1, s32[8,128]{1,0:T(8,128)} %bitcast.4, s32[8,128]{1,0:T(8,128)} %bitcast.5), custom_call_target="tpu_custom_call" | custom-call | tf_op jit(solution)/shard_map/pallas_call | solution.py:389
  50.3 0.6 %copy.5 = f32[1024]{0:T(1024)} copy(f32[1024]{0:T(1024)S(1)} %bitcast.3) | data formatting | bytes 8192

commit v4 on v3

--- a/solution.py
+++ b/solution.py
@@ -12,11 +12,13 @@
 LANES = 128
 GROUP = 2 * LANES
 LEAD = 4
+PLANE = 16
+OVER = 2
 OUT = -4.0
 
 
 def kernel(n_slab, n_member, x_ref, ids_ref, keep_ref, out_ref, raw, blk, tags, pres, qacc, msg, got,
-           load_sem, send_sem, recv_sem, tag_send, tag_recv, msg_send, msg_recv):
+           relay, load_sem, send_sem, recv_sem, tag_send, tag_recv, msg_send, msg_recv, over_send, over_recv, ready):
     rows, width = raw.shape
     chunks, groups = rows // LANES, rows // GROUP
     count = n_slab * n_member
@@ -36,13 +38,21 @@
     has_second = (even & has_up) | (odd & has_down)
     has_a, has_b, has_c = has_second, has_first, even | has_up
     gives_c = odd | has_up
+    step_at = lax.rem(chip, PLANE)
+    over_r, over_l = odd & (step_at == 0) & has_down, odd & (step_at == PLANE - 1) & has_up
+    over_y = odd & (chip == count // 2 - 1)
+    crossings = count // 2 // PLANE - 1
+    crossing = lax.div(chip + 1, PLANE) - 1
+    over_first, over_next = over_r & (crossing == 0), over_r & (crossing == 1)
+    over_to_y = over_r & jnp.logical_not(over_first)
     c_source = jnp.where(even, A, OWN)
     sibling = (slab, member + 1 - 2 * core)
     above, below = device(place + 1), device(place - 1)
 
     barrier = pltpu.get_barrier_semaphore()
     partners = ((has_first, first), (has_second, second), (place < count - 1, above), (place > 0, below))
-    for there, other in partners:
+    told = partners + ((over_to_y | over_l, device(count - 1)), (over_next, device(place - 2 * PLANE)))
+    for there, other in told:
         @pl.when(there)
         def _():
             pl.semaphore_signal(barrier, inc=1, device_id=other, device_id_type=MESH)
@@ -99,7 +109,14 @@
     load_ids.wait()
     load_keep.wait()
     tags[OWN, chunks:2 * chunks] = jnp.where(tags[OWN, chunks:2 * chunks] == 1, tags[OWN, 0:chunks], -1)
-    pl.semaphore_wait(barrier, sum(there.astype(jnp.int32) for there, _ in partners))
+    heard = sum(there.astype(jnp.int32) for there, _ in partners)
+    heard = heard + over_first.astype(jnp.int32) + over_y.astype(jnp.int32) * (2 * crossings - 1)
+    pl.semaphore_wait(barrier, heard)
+
+    @pl.when(over_y)
+    def _():
+        for i in range(1, crossings):
+            pl.semaphore_signal(ready, inc=1, device_id=device(2 * PLANE * (i + 1) + 1), device_id_type=MESH)
 
     @pl.when(has_first)
     def _():
@@ -189,15 +206,38 @@
             best = tile_pair(p, p_bias, best, q_slot, g, cluster, q_at)
         keep_rows(p_slot, t, size, best)
 
-    def some(p_slot, g, q_slot, arrivals, cluster, q_at):
-        p = blk[p_slot, group_at(g), :]
-        p_bias = biases(p_slot, 2 * g, 2, cluster)
-        best = jnp.full((GROUP, LANES), OUT, jnp.float32)
+    def some(p_slot, t, size, q_slot, arrivals, cluster, q_at):
+        p = blk[p_slot, pl.ds(pl.multiple_of(t * LANES, LANES), size * LANES), :]
+        p_bias = biases(p_slot, t, size, cluster)
+        best = jnp.full((size * LANES, LANES), OUT, jnp.float32)
         for i in arrivals:
             best = tile_pair(p, p_bias, best, q_slot, order(q_slot, i, groups), cluster, q_at)
-        keep_rows(p_slot, 2 * g, 2, best)
+        keep_rows(p_slot, t, size, best)
 
     lax.fori_loop(0, groups, own_step, 0)
+
+    over_target = device(jnp.where(crossing == 0, place + 2 * PLANE, count - 1))
+
+    def over_l_at(i):
+        return device(2 * (PLANE * (i + 1) - 1) + 1)
+
+    def over(i, t, way, target):
+        source, there = way
+        rows_of = part(chunks - OVER + t)
+        return pltpu.make_async_remote_copy(
+            src_ref=relay.at[i, t] if source is relay else blk.at[OWN, rows_of],
+            dst_ref=relay.at[i, t] if there is relay else blk.at[B, rows_of],
+            send_sem=over_send.at[i, t], recv_sem=over_recv.at[i, t] if there is relay else recv_sem.at[B, chunks - OVER + t],
+            device_id=target, device_id_type=MESH)
+
+    @pl.when(over_to_y)
+    def _():
+        pl.semaphore_wait(ready, 1)
+
+    @pl.when(over_r)
+    def _():
+        for t in range(OVER):
+            over(crossing, t, (OWN, relay), over_target).start()
 
     @pl.when(has_first)
     def _():
@@ -206,8 +246,19 @@
 
     @pl.when(has_second)
     def _():
-        for t in range(chunks):
+        for t in range(chunks - OVER):
             send(B, t).start()
+
+    @pl.when(has_second & jnp.logical_not(over_r))
+    def _():
+        for t in range(chunks - OVER, chunks):
+            send(B, t).start()
+
+    @pl.when(over_next)
+    def _():
+        for t in range(OVER):
+            over(0, t, (OWN, relay), first).wait_recv()
+            over(0, t, (relay, relay), over_target).start()
 
     @pl.when(has_first)
     def _():
@@ -242,6 +293,13 @@
             send(C, t).wait_recv()
 
     def step(j, _):
+        @pl.when(over_y & (j == groups - 1))
+        def _():
+            for i in range(crossings):
+                for t in range(OVER):
+                    over(i, t, (OWN, relay), first).wait_recv()
+                    over(i, t, (relay, B), over_l_at(i)).start()
+
         @pl.when(has_a)
         def _():
             send(A, 2 * j).wait_recv()
@@ -268,9 +326,9 @@
         for now in range(groups):
             @pl.when(odd & has_a & has_c & (j == now))
             def _():
-                some(C, now, A, range(now + 1), s_c, 4)
+                some(C, 2 * now, 2, A, range(now + 1), s_c, 4)
                 if now > 0:
-                    some(A, order(A, now, groups), C, range(now), s_a, 5)
+                    some(A, 2 * order(A, now, groups), 2, C, range(now), s_a, 5)
 
         m = j - 1
 
@@ -286,7 +344,7 @@
             for now in range(groups - 1):
                 @pl.when(has_a & (m == now))
                 def _():
-                    some(B, order(B, now, groups), A, range(min(now + 2, groups - now)), s_b, 3)
+                    some(B, 2 * order(B, now, groups), 2, A, range(min(now + 2, groups - now)), s_b, 3)
 
         return 0
 
@@ -298,47 +356,69 @@
             recv_sem=msg_recv.at[which], device_id=target, device_id_type=MESH)
 
     def masked(slot, tile, cluster, values):
-        lanes = slice(tile * LANES, (tile + 1) * LANES)
-        best = jnp.max(values[:, lanes], axis=0, keepdims=True)
-        return jnp.where(row(slot, tile) == cluster, best, -1.0)
+        return jnp.where(row(slot, tile) == cluster, jnp.max(values, axis=0, keepdims=True), -1.0)
+
+    def message_a(tile):
+        msg[0, pl.ds(tile, 1), :] = jnp.maximum(
+            jnp.maximum(masked(A, tile, s_a, pres[0, :, part(tile)]), masked(A, tile, s_b, qacc[3, :, part(tile)])),
+            jnp.where(odd, masked(A, tile, s_c, qacc[4, :, part(tile)]), -1.0))
+
+    def message_b(tile):
+        msg[1, pl.ds(tile, 1), :] = masked(B, tile, s_b, pres[1, :, part(tile)])
+
+    for tile in range(chunks):
+        msg[2, tile:tile + 1, :] = jnp.maximum(
+            masked(C, tile, s_c, pres[2, :, part(tile)]), jnp.where(odd, masked(C, tile, s_a, qacc[5, :, part(tile)]), -1.0))
 
     @pl.when(odd & has_c)
     def _():
-        for tile in range(chunks):
-            msg[2, tile:tile + 1, :] = jnp.maximum(masked(C, tile, s_c, pres[2]), masked(C, tile, s_a, qacc[5]))
         message(2, above).start()
 
+    for tile in range(chunks):
+        own = jnp.max(qacc[0, :, part(tile)], axis=0, keepdims=True)
+        out_ref[tile:tile + 1, :] = jnp.maximum(
+            jnp.maximum(own, -1.0),
+            jnp.maximum(masked(OWN, tile, s_a, qacc[1, :, part(tile)]), masked(OWN, tile, s_c, qacc[2, :, part(tile)])))
+
     @pl.when(has_a & has_b)
     def _():
-        some(B, order(B, 0, groups), A, range(2, groups), s_b, 3)
+        some(B, 2 * order(B, 0, groups), 2, A, range(2, groups), s_b, 3)
+
+    for t in range(2, chunks):
+        message_a(order(A, t, chunks))
+    for t in range(chunks - 2):
+        message_b(order(B, t, chunks))
 
     def last_step(t, _):
         @pl.when(has_b)
         def _():
             send(B, t).wait_recv()
 
+        @pl.when(has_a & has_b)
+        def _():
+            some(B, order(B, t, chunks), 1, A, range(1), s_b, 3)
+
+        @pl.when(t == chunks - 1)
+        def _():
+            for i in range(2):
+                message_a(order(A, i, chunks))
+
+            @pl.when(has_a)
+            def _():
+                message(0, second).start()
+
         @pl.when(even & has_b)
         def _():
             whole(B, order(B, t, chunks), 1, C, s_b, 4)
 
+        @pl.when(has_b)
+        def _():
+            message_b(order(B, t, chunks))
+
         return 0
 
     lax.fori_loop(chunks - 2, chunks, last_step, 0)
 
-    @pl.when(has_a & has_b)
-    def _():
-        some(B, order(B, groups - 1, groups), A, range(1), s_b, 3)
-
-    for tile in range(chunks):
-        msg[0, tile:tile + 1, :] = jnp.maximum(
-            jnp.maximum(masked(A, tile, s_a, pres[0]), masked(A, tile, s_b, qacc[3])),
-            jnp.where(odd, masked(A, tile, s_c, qacc[4]), -1.0))
-        msg[1, tile:tile + 1, :] = masked(B, tile, s_b, pres[1])
-
-    @pl.when(has_a)
-    def _():
-        message(0, second).start()
-
     @pl.when(has_b)
     def _():
         message(1, first).start()
@@ -346,17 +426,11 @@
     @pl.when(even)
     def _():
         for tile in range(chunks):
-            msg[2, tile:tile + 1, :] = jnp.maximum(masked(C, tile, s_c, pres[2]), masked(C, tile, s_b, qacc[4]))
+            msg[2, tile:tile + 1, :] = jnp.maximum(
+                msg[2, tile:tile + 1, :], masked(C, tile, s_b, qacc[4, :, part(tile)]))
         message(2, above).start()
 
     messages = ((has_a, second, has_first), (has_b, first, has_second), (has_c, above, odd | has_down))
-    for tile in range(chunks):
-        lanes = slice(tile * LANES, (tile + 1) * LANES)
-        own = jnp.max(qacc[0, :, lanes], axis=0, keepdims=True)
-        out_ref[tile:tile + 1, :] = jnp.maximum(
-            jnp.maximum(own, -1.0),
-            jnp.maximum(masked(OWN, tile, s_a, qacc[1]), masked(OWN, tile, s_c, qacc[2])))
-
     @pl.when(has_first)
     def _():
         for t in range(LEAD, chunks):
@@ -364,8 +438,29 @@
 
     @pl.when(has_second)
     def _():
-        for t in range(chunks):
+        for t in range(chunks - OVER):
             send(B, t).wait_send()
+
+    @pl.when(has_second & jnp.logical_not(over_r))
+    def _():
+        for t in range(chunks - OVER, chunks):
+            send(B, t).wait_send()
+
+    @pl.when(over_r)
+    def _():
+        for t in range(OVER):
+            over(crossing, t, (OWN, relay), over_target).wait_send()
+
+    @pl.when(over_next)
+    def _():
+        for t in range(OVER):
+            over(0, t, (relay, relay), over_target).wait_send()
+
+    @pl.when(over_y)
+    def _():
+        for i in range(crossings):
+            for t in range(OVER):
+                over(i, t, (relay, B), over_l_at(i)).wait_send()
 
     @pl.when(gives_c)
     def _():
@@ -386,6 +481,7 @@
 def shards(n_slab, n_member, embeddings, cluster_ids, keep_mask):
     rows, width = embeddings.shape
     chunks = rows // LANES
+    crossings = n_slab * n_member // 2 // PLANE - 1
     highest = pl.pallas_call(
         functools.partial(kernel, n_slab, n_member),
         out_shape=jax.ShapeDtypeStruct((chunks, LANES), jnp.float32),
@@ -399,6 +495,7 @@
             pltpu.VMEM((6, 8, rows), jnp.float32),
             pltpu.VMEM((3, chunks, LANES), jnp.float32),
             pltpu.VMEM((3, chunks, LANES), jnp.float32),
+            pltpu.VMEM((crossings, OVER, LANES, width), jnp.bfloat16),
             pltpu.SemaphoreType.DMA((chunks + 2,)),
             pltpu.SemaphoreType.DMA((4, chunks)),
             pltpu.SemaphoreType.DMA((4, chunks)),
@@ -406,6 +503,9 @@
             pltpu.SemaphoreType.DMA((4,)),
             pltpu.SemaphoreType.DMA((3,)),
             pltpu.SemaphoreType.DMA((3,)),
+            pltpu.SemaphoreType.DMA((crossings, OVER)),
+            pltpu.SemaphoreType.DMA((crossings, OVER)),
+            pltpu.SemaphoreType.REGULAR,
         ],
         compiler_params=pltpu.CompilerParams(
             collective_id=0, has_side_effects=True, vmem_limit_bytes=40 << 20),

time: 51 us -> 48.6 us (0.953)
  Pallas kernels: 50.3 us -> 47.9 us
    pallas_call x1, Pallas kernels: 50.3 us -> 47.9 us  [shards(): pl.pallas_call(functools.partial(kernel, n_slab, n_member), out_shape=jax...]
where the time goes in v4:
time: 48.6 us; the launch traced here: 48.5 us
  Pallas kernels  47.9 us (99%)
  local copies, waits for them, and re-layouts  0.6 us (1%)
    pallas_call x1, Pallas kernels, shards(): pl.pallas_call(functools.partial(kernel, n_slab, n_member), out_shape=jax...  47.9 us

profile of v4, /device:TPU:7, one launch (start us, length us, event | category | flops | bytes accessed | tf_op | source)
XLA Modules:
  0.0 48.5 jit_solution(6480100729159351676)
XLA Ops:
  0.0 47.9 %shard_map.37 = f32[8,128]{1,0:T(8,128)S(1)} custom-call(bf16[1024,768]{1,0:T(8,128)(2,1)} %x_ref.1, s32[8,128]{1,0:T(8,128)} %bitcast.4, s32[8,128]{1,0:T(8,128)} %bitcast.5), custom_call_target="tpu_custom_call" | custom-call | tf_op jit(solution)/shard_map/pallas_call | solution.py:485
  47.9 0.6 %copy.5 = f32[1024]{0:T(1024)} copy(f32[1024]{0:T(1024)S(1)} %bitcast.3) | data formatting | bytes 8192

commit v5 on v4

--- a/solution.py
+++ b/solution.py
@@ -11,9 +11,9 @@
 OWN, A, B, C = 0, 1, 2, 3
 LANES = 128
 GROUP = 2 * LANES
-LEAD = 4
+LEAD = 5
 PLANE = 16
-OVER = 2
+OVER = 3
 OUT = -4.0
 
 
@@ -214,8 +214,6 @@
             best = tile_pair(p, p_bias, best, q_slot, order(q_slot, i, groups), cluster, q_at)
         keep_rows(p_slot, t, size, best)
 
-    lax.fori_loop(0, groups, own_step, 0)
-
     over_target = device(jnp.where(crossing == 0, place + 2 * PLANE, count - 1))
 
     def over_l_at(i):
@@ -230,29 +228,18 @@
             send_sem=over_send.at[i, t], recv_sem=over_recv.at[i, t] if there is relay else recv_sem.at[B, chunks - OVER + t],
             device_id=target, device_id_type=MESH)
 
-    @pl.when(over_to_y)
-    def _():
-        pl.semaphore_wait(ready, 1)
-
-    @pl.when(over_r)
+    @pl.when(over_first)
     def _():
         for t in range(OVER):
             over(crossing, t, (OWN, relay), over_target).start()
 
-    @pl.when(has_first)
-    def _():
-        for t in range(LEAD):
-            send(A, t).wait_send()
-
-    @pl.when(has_second)
-    def _():
-        for t in range(chunks - OVER):
-            send(B, t).start()
-
-    @pl.when(has_second & jnp.logical_not(over_r))
-    def _():
-        for t in range(chunks - OVER, chunks):
-            send(B, t).start()
+    lax.fori_loop(0, groups, own_step, 0)
+
+    @pl.when(over_to_y)
+    def _():
+        pl.semaphore_wait(ready, 1)
+        for t in range(OVER):
+            over(crossing, t, (OWN, relay), over_target).start()
 
     @pl.when(over_next)
     def _():
@@ -262,6 +249,21 @@
 
     @pl.when(has_first)
     def _():
+        for t in range(LEAD):
+            send(A, t).wait_send()
+
+    @pl.when(has_second)
+    def _():
+        for t in range(chunks - OVER):
+            send(B, t).start()
+
+    @pl.when(has_second & jnp.logical_not(over_r))
+    def _():
+        for t in range(chunks - OVER, chunks):
+            send(B, t).start()
+
+    @pl.when(has_first)
+    def _():
         send_tags(OWN, A, first).wait_send()
 
     @pl.when(has_second)
@@ -293,7 +295,7 @@
             send(C, t).wait_recv()
 
     def step(j, _):
-        @pl.when(over_y & (j == groups - 1))
+        @pl.when(over_y & (j == groups - 2))
         def _():
             for i in range(crossings):
                 for t in range(OVER):

time: 48.6 us -> 47.7 us (0.981)
  Pallas kernels: 47.9 us -> 46.9 us
    pallas_call x1, Pallas kernels: 47.9 us -> 46.9 us  [shards(): pl.pallas_call(functools.partial(kernel, n_slab, n_member), out_shape=jax...]
where the time goes in v5:
time: 47.7 us; the launch traced here: 47.5 us
  Pallas kernels  46.9 us (98%)
  local copies, waits for them, and re-layouts  0.6 us (1%)
    pallas_call x1, Pallas kernels, shards(): pl.pallas_call(functools.partial(kernel, n_slab, n_member), out_shape=jax...  46.9 us

profile of v5, /device:TPU:7, one launch (start us, length us, event | category | flops | bytes accessed | tf_op | source)
XLA Modules:
  0.0 47.5 jit_solution(6923315617210359897)
XLA Ops:
  0.0 46.9 %shard_map.37 = f32[8,128]{1,0:T(8,128)S(1)} custom-call(bf16[1024,768]{1,0:T(8,128)(2,1)} %x_ref.1, s32[8,128]{1,0:T(8,128)} %bitcast.4, s32[8,128]{1,0:T(8,128)} %bitcast.5), custom_call_target="tpu_custom_call" | custom-call | tf_op jit(solution)/shard_map/pallas_call | solution.py:487
  46.9 0.6 %copy.5 = f32[1024]{0:T(1024)} copy(f32[1024]{0:T(1024)S(1)} %bitcast.3) | data formatting | bytes 8192

commit v6 on v5

--- a/solution.py
+++ b/solution.py
@@ -12,13 +12,15 @@
 LANES = 128
 GROUP = 2 * LANES
 LEAD = 5
+MORE = 2
 PLANE = 16
-OVER = 3
+DOWN, UP = 3, 1
 OUT = -4.0
 
 
 def kernel(n_slab, n_member, x_ref, ids_ref, keep_ref, out_ref, raw, blk, tags, pres, qacc, msg, got,
-           relay, load_sem, send_sem, recv_sem, tag_send, tag_recv, msg_send, msg_recv, over_send, over_recv, ready):
+           relay, load_sem, send_sem, recv_sem, tag_send, tag_recv, msg_send, msg_recv, over_send, over_recv, ready, early,
+           edge_rows, edge_tags, edge_out, edge_got, edge_send, edge_recv):
     rows, width = raw.shape
     chunks, groups = rows // LANES, rows // GROUP
     count = n_slab * n_member
@@ -43,16 +45,29 @@
     over_y = odd & (chip == count // 2 - 1)
     crossings = count // 2 // PLANE - 1
     crossing = lax.div(chip + 1, PLANE) - 1
+    is_r, above_r = (step_at == 0) & has_down, (step_at == 1) & (chip > PLANE)
     over_first, over_next = over_r & (crossing == 0), over_r & (crossing == 1)
     over_to_y = over_r & jnp.logical_not(over_first)
+    up_r, up_l = even & (step_at == 0) & has_down, even & (step_at == PLANE - 1) & has_up
+    up_y = even & (chip == 0)
+    up_mid, up_far = up_r & (crossing == 0), up_r & (crossing == 1)
+    edge = even & (step_at == PLANE - 2) & (chip < count // 2 - PLANE)
+    up_last, up_pass = up_l & (crossing == 2), up_l & (crossing == 1)
     c_source = jnp.where(even, A, OWN)
     sibling = (slab, member + 1 - 2 * core)
     above, below = device(place + 1), device(place - 1)
 
     barrier = pltpu.get_barrier_semaphore()
     partners = ((has_first, first), (has_second, second), (place < count - 1, above), (place > 0, below))
-    told = partners + ((over_to_y | over_l, device(count - 1)), (over_next, device(place - 2 * PLANE)))
-    for there, other in told:
+    told = partners + ((over_to_y | over_l, device(count - 1)), (over_next | up_far, device(place - 2 * PLANE)), (up_r & jnp.logical_not(up_far), device(0)))
+    told = told + ((up_pass, device(place + 2 * PLANE)),)
+    told = told + tuple((up_y, device(2 * (PLANE * (i + 1) - 1))) for i in range(crossings - 1))
+    for there, other in told[:2]:
+        @pl.when(there & jnp.logical_not(above_r & (odd if other is second else even)))
+        def _():
+            pl.semaphore_signal(barrier, inc=1, device_id=other, device_id_type=MESH)
+
+    for there, other in told[2:]:
         @pl.when(there)
         def _():
             pl.semaphore_signal(barrier, inc=1, device_id=other, device_id_type=MESH)
@@ -111,26 +126,41 @@
     tags[OWN, chunks:2 * chunks] = jnp.where(tags[OWN, chunks:2 * chunks] == 1, tags[OWN, 0:chunks], -1)
     heard = sum(there.astype(jnp.int32) for there, _ in partners)
     heard = heard + over_first.astype(jnp.int32) + over_y.astype(jnp.int32) * (2 * crossings - 1)
-    pl.semaphore_wait(barrier, heard)
+    heard = heard + (up_l | up_mid).astype(jnp.int32) + up_y.astype(jnp.int32) * (crossings - 1)
+    heard = heard - is_r.astype(jnp.int32)
+
+    @pl.when(jnp.logical_not(is_r))
+    def _():
+        pl.semaphore_wait(barrier, heard)
+
+    @pl.when(above_r)
+    def _():
+        pl.semaphore_signal(early, inc=1, device_id=device(place - 2), device_id_type=MESH)
+
+    @pl.when(is_r)
+    def _():
+        pl.semaphore_wait(early, 1)
 
     @pl.when(over_y)
     def _():
         for i in range(1, crossings):
             pl.semaphore_signal(ready, inc=1, device_id=device(2 * PLANE * (i + 1) + 1), device_id_type=MESH)
 
-    @pl.when(has_first)
+    first_now, second_now = has_first & jnp.logical_not(is_r & even), has_second & jnp.logical_not(is_r & odd)
+
+    @pl.when(first_now)
     def _():
         send(A, 0).start()
         send_tags(OWN, A, first).start()
 
-    @pl.when(has_second)
+    @pl.when(second_now)
     def _():
         send_tags(OWN, B, second).start()
 
     def prepare(t, _):
         normalise(order(A, t, chunks))
 
-        @pl.when(has_first)
+        @pl.when(first_now)
         def _():
             send(A, t).start()
 
@@ -138,7 +168,7 @@
 
     lax.fori_loop(1, chunks, prepare, 0)
 
-    @pl.when(odd)
+    @pl.when(odd & jnp.logical_not(is_r))
     def _():
         for t in range(chunks):
             send(C, t).start()
@@ -214,52 +244,94 @@
             best = tile_pair(p, p_bias, best, q_slot, order(q_slot, i, groups), cluster, q_at)
         keep_rows(p_slot, t, size, best)
 
-    over_target = device(jnp.where(crossing == 0, place + 2 * PLANE, count - 1))
-
-    def over_l_at(i):
-        return device(2 * (PLANE * (i + 1) - 1) + 1)
-
-    def over(i, t, way, target):
+    over_target = device(jnp.where(even, jnp.where(up_last, place - 2 * PLANE, 0), jnp.where(crossing == 0, place + 2 * PLANE, count - 1)))
+
+    def l_at(i):
+        return device(2 * (PLANE * (i + 1) - 1) + core)
+
+    def r_at(i):
+        return device(2 * PLANE * (i + 1) + core)
+
+    def over(total, i, t, way, target):
         source, there = way
-        rows_of = part(chunks - OVER + t)
+        rows_of = part(order(B, chunks - total + t, chunks))
         return pltpu.make_async_remote_copy(
             src_ref=relay.at[i, t] if source is relay else blk.at[OWN, rows_of],
             dst_ref=relay.at[i, t] if there is relay else blk.at[B, rows_of],
-            send_sem=over_send.at[i, t], recv_sem=over_recv.at[i, t] if there is relay else recv_sem.at[B, chunks - OVER + t],
+            send_sem=over_send.at[i, t],
+            recv_sem=over_recv.at[i, t] if there is relay else recv_sem.at[B, chunks - total + t],
             device_id=target, device_id_type=MESH)
 
+    @pl.when(up_l)
+    def _():
+        for t in range(UP):
+            over(UP, crossing, t, (OWN, relay), over_target).start()
+
+    lax.fori_loop(0, groups, own_step, 0)
+
+    @pl.when(is_r)
+    def _():
+        pl.semaphore_wait(barrier, heard)
+
+    @pl.when(is_r & even)
+    def _():
+        send_tags(OWN, A, first).start()
+        for t in range(chunks):
+            send(A, t).start()
+
+    @pl.when(is_r & odd)
+    def _():
+        send_tags(OWN, B, second).start()
+        for t in range(chunks):
+            send(C, t).start()
+
     @pl.when(over_first)
     def _():
-        for t in range(OVER):
-            over(crossing, t, (OWN, relay), over_target).start()
-
-    lax.fori_loop(0, groups, own_step, 0)
+        for t in range(DOWN):
+            over(DOWN, crossing, t, (OWN, relay), over_target).start()
+
 
     @pl.when(over_to_y)
     def _():
         pl.semaphore_wait(ready, 1)
-        for t in range(OVER):
-            over(crossing, t, (OWN, relay), over_target).start()
+        for t in range(DOWN):
+            over(DOWN, crossing, t, (OWN, relay), over_target).start()
+
+    @pl.when(up_pass)
+    def _():
+        for t in range(UP):
+            over(UP, 2, t, (OWN, relay), first).wait_recv()
+            over(UP, 2, t, (relay, relay), over_target).start()
 
     @pl.when(over_next)
     def _():
-        for t in range(OVER):
-            over(0, t, (OWN, relay), first).wait_recv()
-            over(0, t, (relay, relay), over_target).start()
+        for t in range(DOWN):
+            over(DOWN, 0, t, (OWN, relay), first).wait_recv()
+            over(DOWN, 0, t, (relay, relay), over_target).start()
 
     @pl.when(has_first)
     def _():
         for t in range(LEAD):
             send(A, t).wait_send()
 
+    @pl.when(is_r & odd)
+    def _():
+        for t in range(LEAD, LEAD + MORE):
+            send(A, t).wait_send()
+
     @pl.when(has_second)
     def _():
-        for t in range(chunks - OVER):
+        for t in range(chunks - DOWN):
             send(B, t).start()
 
     @pl.when(has_second & jnp.logical_not(over_r))
     def _():
-        for t in range(chunks - OVER, chunks):
+        for t in range(chunks - DOWN, chunks - UP):
+            send(B, t).start()
+
+    @pl.when(has_second & jnp.logical_not(over_r | up_l))
+    def _():
+        for t in range(chunks - UP, chunks):
             send(B, t).start()
 
     @pl.when(has_first)
@@ -294,13 +366,40 @@
         for t in range(chunks):
             send(C, t).wait_recv()
 
+    def edge_copies():
+        return (
+            pltpu.make_async_remote_copy(
+                src_ref=blk.at[A, part(0)], dst_ref=edge_rows, send_sem=edge_send.at[0], recv_sem=edge_recv.at[0],
+                device_id=first, device_id_type=MESH),
+            pltpu.make_async_remote_copy(
+                src_ref=tags.at[A], dst_ref=edge_tags, send_sem=edge_send.at[1], recv_sem=edge_recv.at[1],
+                device_id=first, device_id_type=MESH))
+
+    def edge_message():
+        return pltpu.make_async_remote_copy(
+            src_ref=edge_out, dst_ref=edge_got, send_sem=edge_send.at[2], recv_sem=edge_recv.at[2],
+            device_id=second, device_id_type=MESH)
+
     def step(j, _):
-        @pl.when(over_y & (j == groups - 2))
+        @pl.when(up_mid & (j == groups - 1))
+        def _():
+            for t in range(UP):
+                over(UP, 1, t, (OWN, relay), first).wait_recv()
+                over(UP, 1, t, (relay, B), r_at(1)).start()
+
+        @pl.when(over_y & (j == groups - 3))
         def _():
             for i in range(crossings):
-                for t in range(OVER):
-                    over(i, t, (OWN, relay), first).wait_recv()
-                    over(i, t, (relay, B), over_l_at(i)).start()
+                for t in range(DOWN):
+                    over(DOWN, i, t, (OWN, relay), first).wait_recv()
+                    over(DOWN, i, t, (relay, B), l_at(i)).start()
+
+        @pl.when(up_y & (j == groups - 2))
+        def _():
+            for i in (1, 0, 2):
+                for t in range(UP):
+                    over(UP, i, t, (OWN, relay), first).wait_recv()
+                    over(UP, i, t, (relay, relay if i == 1 else B), r_at(0 if i == 1 else i)).start()
 
         @pl.when(has_a)
         def _():
@@ -311,6 +410,11 @@
         def _():
             send(C, 2 * j).start()
             send(C, 2 * j + 1).start()
+
+        @pl.when(up_l & (j == 0))
+        def _():
+            for each in edge_copies():
+                each.start()
 
         @pl.when(has_a)
         def _():
@@ -334,7 +438,7 @@
 
         m = j - 1
 
-        @pl.when(has_b & (j > 0))
+        @pl.when(has_b & (j > 0) & (j < groups - 1))
         def _():
             send(B, 2 * m).wait_recv()
             send(B, 2 * m + 1).wait_recv()
@@ -343,7 +447,7 @@
             def _():
                 whole(B, 2 * order(B, m, groups), 2, C, s_b, 4)
 
-            for now in range(groups - 1):
+            for now in range(groups - 2):
                 @pl.when(has_a & (m == now))
                 def _():
                     some(B, 2 * order(B, now, groups), 2, A, range(min(now + 2, groups - now)), s_b, 3)
@@ -382,28 +486,92 @@
             jnp.maximum(own, -1.0),
             jnp.maximum(masked(OWN, tile, s_a, qacc[1, :, part(tile)]), masked(OWN, tile, s_c, qacc[2, :, part(tile)])))
 
+    @pl.when(edge)
+    def _():
+        for each in edge_copies():
+            each.wait_recv()
+        cluster = edge_tags[0:1, 0:1]
+        s = lax.dot_general(
+            edge_rows[...], blk[OWN, part(0), :], (((1,), (1,)), ((), ())), preferred_element_type=jnp.float32)
+        p_bias = columns(jnp.where(edge_tags[chunks:chunks + 1, :] == cluster, 0.0, OUT))
+        q_bias = jnp.where(row(OWN, chunks) == cluster, 0.0, OUT)
+        rows_best = jnp.max((s + q_bias).T, axis=0, keepdims=True)
+        edge_out[...] = jnp.broadcast_to(jnp.where(edge_tags[0:1, :] == cluster, rows_best, -1.0), edge_out.shape)
+        edge_message().start()
+        own_best = jnp.max(s + p_bias, axis=0, keepdims=True)
+        out_ref[0:1, :] = jnp.maximum(out_ref[0:1, :], jnp.where(row(OWN, 0) == cluster, own_best, -1.0))
+
     @pl.when(has_a & has_b)
     def _():
         some(B, 2 * order(B, 0, groups), 2, A, range(2, groups), s_b, 3)
 
-    for t in range(2, chunks):
+    for t in range(4, chunks):
         message_a(order(A, t, chunks))
-    for t in range(chunks - 2):
+    for t in range(chunks - 4):
         message_b(order(B, t, chunks))
 
-    def last_step(t, _):
-        @pl.when(has_b)
-        def _():
+    @pl.when(over_l)
+    def _():
+        for t in range(chunks - 2, chunks):
             send(B, t).wait_recv()
-
-        @pl.when(has_a & has_b)
+        some(B, 2 * order(B, groups - 1, groups), 2, A, range(1), s_b, 3)
+        for t in range(chunks - 2, chunks):
+            message_b(order(B, t, chunks))
+
+    @pl.when(has_b)
+    def _():
+        m = groups - 2
+        send(B, 2 * m).wait_recv()
+        send(B, 2 * m + 1).wait_recv()
+
+        @pl.when(has_a)
+        def _():
+            some(B, 2 * order(B, m, groups), 2, A, range(groups - m), s_b, 3)
+
+        @pl.when(even)
+        def _():
+            whole(B, 2 * order(B, m, groups), 2, C, s_b, 4)
+
+    for t in range(chunks - 4, chunks - 2):
+        message_b(order(B, t, chunks))
+
+    @pl.when(over_l)
+    def _():
+        message(1, first).start()
+
+    for t in range(2, 4):
+        message_a(order(A, t, chunks))
+
+    def last_step(i, _):
+        t = i + up_r.astype(jnp.int32) * (2 * chunks - 3 - 2 * i)
+
+        comes = has_b & jnp.logical_not(over_l)
+
+        @pl.when(comes)
+        def _():
+            send(B, t).wait_recv()
+
+        @pl.when(has_a & comes)
         def _():
             some(B, order(B, t, chunks), 1, A, range(1), s_b, 3)
 
-        @pl.when(t == chunks - 1)
-        def _():
-            for i in range(2):
-                message_a(order(A, i, chunks))
+        @pl.when(odd & comes)
+        def _():
+            message_b(order(B, t, chunks))
+
+        @pl.when(odd & comes & (i == chunks - 1))
+        def _():
+            message(1, first).start()
+
+        @pl.when(i == jnp.where(up_l, chunks - 2, chunks - 1))
+        def _():
+            for each in range(2):
+                message_a(order(A, each, chunks))
+
+            @pl.when(up_l)
+            def _():
+                edge_message().wait_recv()
+                msg[0, 0:1, :] = jnp.maximum(msg[0, 0:1, :], edge_got[0:1, :])
 
             @pl.when(has_a)
             def _():
@@ -413,7 +581,7 @@
         def _():
             whole(B, order(B, t, chunks), 1, C, s_b, 4)
 
-        @pl.when(has_b)
+        @pl.when(even & has_b)
         def _():
             message_b(order(B, t, chunks))
 
@@ -421,7 +589,7 @@
 
     lax.fori_loop(chunks - 2, chunks, last_step, 0)
 
-    @pl.when(has_b)
+    @pl.when(even & has_b)
     def _():
         message(1, first).start()
 
@@ -435,39 +603,79 @@
     messages = ((has_a, second, has_first), (has_b, first, has_second), (has_c, above, odd | has_down))
     @pl.when(has_first)
     def _():
-        for t in range(LEAD, chunks):
+        for t in range(LEAD + MORE, chunks):
             send(A, t).wait_send()
 
+    @pl.when(has_first & jnp.logical_not(is_r & odd))
+    def _():
+        for t in range(LEAD, LEAD + MORE):
+            send(A, t).wait_send()
+
     @pl.when(has_second)
     def _():
-        for t in range(chunks - OVER):
+        for t in range(chunks - DOWN):
             send(B, t).wait_send()
 
     @pl.when(has_second & jnp.logical_not(over_r))
     def _():
-        for t in range(chunks - OVER, chunks):
+        for t in range(chunks - DOWN, chunks - UP):
             send(B, t).wait_send()
 
+    @pl.when(has_second & jnp.logical_not(over_r | up_l))
+    def _():
+        for t in range(chunks - UP, chunks):
+            send(B, t).wait_send()
+
     @pl.when(over_r)
     def _():
-        for t in range(OVER):
-            over(crossing, t, (OWN, relay), over_target).wait_send()
+        for t in range(DOWN):
+            over(DOWN, crossing, t, (OWN, relay), over_target).wait_send()
 
     @pl.when(over_next)
     def _():
-        for t in range(OVER):
-            over(0, t, (relay, relay), over_target).wait_send()
+        for t in range(DOWN):
+            over(DOWN, 0, t, (relay, relay), over_target).wait_send()
 
     @pl.when(over_y)
     def _():
         for i in range(crossings):
-            for t in range(OVER):
-                over(i, t, (relay, B), over_l_at(i)).wait_send()
+            for t in range(DOWN):
+                over(DOWN, i, t, (relay, B), l_at(i)).wait_send()
+
+    @pl.when(up_l)
+    def _():
+        for t in range(UP):
+            over(UP, crossing, t, (OWN, relay), over_target).wait_send()
+
+    @pl.when(up_pass)
+    def _():
+        for t in range(UP):
+            over(UP, 2, t, (relay, relay), over_target).wait_send()
+
+    @pl.when(up_mid)
+    def _():
+        for t in range(UP):
+            over(UP, 1, t, (relay, B), r_at(1)).wait_send()
+
+    @pl.when(up_y)
+    def _():
+        for i in range(crossings):
+            for t in range(UP):
+                over(UP, i, t, (relay, relay if i == 1 else B), r_at(0 if i == 1 else i)).wait_send()
 
     @pl.when(gives_c)
     def _():
         for t in range(chunks):
             send(C, t).wait_send()
+
+    @pl.when(up_l)
+    def _():
+        for each in edge_copies():
+            each.wait_send()
+
+    @pl.when(edge)
+    def _():
+        edge_message().wait_send()
 
     for which, (gives, target, gets) in enumerate(messages):
         @pl.when(gives)
@@ -497,7 +705,7 @@
             pltpu.VMEM((6, 8, rows), jnp.float32),
             pltpu.VMEM((3, chunks, LANES), jnp.float32),
             pltpu.VMEM((3, chunks, LANES), jnp.float32),
-            pltpu.VMEM((crossings, OVER, LANES, width), jnp.bfloat16),
+            pltpu.VMEM((crossings, DOWN, LANES, width), jnp.bfloat16),
             pltpu.SemaphoreType.DMA((chunks + 2,)),
             pltpu.SemaphoreType.DMA((4, chunks)),
             pltpu.SemaphoreType.DMA((4, chunks)),
@@ -505,9 +713,16 @@
             pltpu.SemaphoreType.DMA((4,)),
             pltpu.SemaphoreType.DMA((3,)),
             pltpu.SemaphoreType.DMA((3,)),
-            pltpu.SemaphoreType.DMA((crossings, OVER)),
-            pltpu.SemaphoreType.DMA((crossings, OVER)),
+            pltpu.SemaphoreType.DMA((crossings, DOWN)),
+            pltpu.SemaphoreType.DMA((crossings, DOWN)),
             pltpu.SemaphoreType.REGULAR,
+            pltpu.SemaphoreType.REGULAR,
+            pltpu.VMEM((LANES, width), jnp.bfloat16),
+            pltpu.VMEM((2 * chunks, LANES), jnp.int32),
+            pltpu.VMEM((8, LANES), jnp.float32),
+            pltpu.VMEM((8, LANES), jnp.float32),
+            pltpu.SemaphoreType.DMA((3,)),
+            pltpu.SemaphoreType.DMA((3,)),
         ],
         compiler_params=pltpu.CompilerParams(
             collective_id=0, has_side_effects=True, vmem_limit_bytes=40 << 20),

time: 47.7 us -> 47.1 us (0.987)
  Pallas kernels: 46.9 us -> 46.3 us
    pallas_call x1, Pallas kernels: 46.9 us -> 46.3 us  [shards(): pl.pallas_call(functools.partial(kernel, n_slab, n_member), out_shape=jax...]
where the time goes in v6:
time: 47.1 us; the launch traced here: 46.9 us
  Pallas kernels  46.3 us (98%)
  local copies, waits for them, and re-layouts  0.6 us (1%)
    pallas_call x1, Pallas kernels, shards(): pl.pallas_call(functools.partial(kernel, n_slab, n_member), out_shape=jax...  46.3 us

profile of v6, /device:TPU:7, one launch (start us, length us, event | category | flops | bytes accessed | tf_op | source)
XLA Modules:
  0.0 46.9 jit_solution(10826641334546217188)
XLA Ops:
  0.0 46.3 %shard_map.37 = f32[8,128]{1,0:T(8,128)S(1)} custom-call(bf16[1024,768]{1,0:T(8,128)(2,1)} %x_ref.1, s32[8,128]{1,0:T(8,128)} %bitcast.4, s32[8,128]{1,0:T(8,128)} %bitcast.5), custom_call_target="tpu_custom_call" | custom-call | tf_op jit(solution)/shard_map/pallas_call | solution.py:695
  46.3 0.6 %copy.5 = f32[1024]{0:T(1024)} copy(f32[1024]{0:T(1024)S(1)} %bitcast.3) | data formatting | bytes 8192

commit v7 on v6

--- a/solution.py
+++ b/solution.py
@@ -267,8 +267,6 @@
         for t in range(UP):
             over(UP, crossing, t, (OWN, relay), over_target).start()
 
-    lax.fori_loop(0, groups, own_step, 0)
-
     @pl.when(is_r)
     def _():
         pl.semaphore_wait(barrier, heard)
@@ -290,6 +288,8 @@
         for t in range(DOWN):
             over(DOWN, crossing, t, (OWN, relay), over_target).start()
 
+
+    lax.fori_loop(0, groups, own_step, 0)
 
     @pl.when(over_to_y)
     def _():

time: 47.1 us -> 47.1 us (level)
  no operation moved by 1% of the time
where the time goes in v7:
time: 47.1 us; the launch traced here: 46.9 us
  Pallas kernels  46.3 us (98%)
  local copies, waits for them, and re-layouts  0.6 us (1%)
    pallas_call x1, Pallas kernels, shards(): pl.pallas_call(functools.partial(kernel, n_slab, n_member), out_shape=jax...  46.3 us

profile of v7, /device:TPU:7, one launch (start us, length us, event | category | flops | bytes accessed | tf_op | source)
XLA Modules:
  0.0 46.9 jit_solution(11588632476012460015)
XLA Ops:
  0.0 46.3 %shard_map.37 = f32[8,128]{1,0:T(8,128)S(1)} custom-call(bf16[1024,768]{1,0:T(8,128)(2,1)} %x_ref.1, s32[8,128]{1,0:T(8,128)} %bitcast.4, s32[8,128]{1,0:T(8,128)} %bitcast.5), custom_call_target="tpu_custom_call" | custom-call | tf_op jit(solution)/shard_map/pallas_call | solution.py:695
  46.3 0.6 %copy.5 = f32[1024]{0:T(1024)} copy(f32[1024]{0:T(1024)S(1)} %bitcast.3) | data formatting | bytes 8192

commit v8 on v7

--- a/solution.py
+++ b/solution.py
@@ -111,8 +111,6 @@
         @pl.when(jnp.logical_not(there))
         def _():
             tags[slot] = jnp.full(tags.shape[1:], -2, jnp.int32)
-    pres[...] = jnp.full(pres.shape, OUT, jnp.float32)
-    qacc[...] = jnp.full(qacc.shape, OUT, jnp.float32)
 
     def normalise(t):
         load(t).wait()
@@ -172,6 +170,9 @@
     def _():
         for t in range(chunks):
             send(C, t).start()
+
+    pres[...] = jnp.full(pres.shape, OUT, jnp.float32)
+    qacc[...] = jnp.full(qacc.shape, OUT, jnp.float32)
 
     def row(slot, t):
         return tags[slot, pl.ds(t, 1), :]
@@ -528,7 +529,7 @@
         def _():
             some(B, 2 * order(B, m, groups), 2, A, range(groups - m), s_b, 3)
 
-        @pl.when(even)
+        @pl.when(even & jnp.logical_not(up_l))
         def _():
             whole(B, 2 * order(B, m, groups), 2, C, s_b, 4)
 
@@ -576,6 +577,12 @@
             @pl.when(has_a)
             def _():
                 message(0, second).start()
+
+            @pl.when(up_l)
+            def _():
+                whole(B, 2 * order(B, groups - 2, groups), 2, C, s_b, 4)
+                for each in range(chunks - 4, chunks - 2):
+                    message_b(order(B, each, chunks))
 
         @pl.when(even & has_b)
         def _():

time: 47.1 us -> 47.1 us (level)
  no operation moved by 1% of the time
where the time goes in v8:
time: 47.1 us; the launch traced here: 46.9 us
  Pallas kernels  46.3 us (98%)
  local copies, waits for them, and re-layouts  0.6 us (1%)
    pallas_call x1, Pallas kernels, shards(): pl.pallas_call(functools.partial(kernel, n_slab, n_member), out_shape=jax...  46.3 us

profile of v8, /device:TPU:7, one launch (start us, length us, event | category | flops | bytes accessed | tf_op | source)
XLA Modules:
  0.0 46.9 jit_solution(2290890732029604753)
XLA Ops:
  0.0 46.3 %shard_map.37 = f32[8,128]{1,0:T(8,128)S(1)} custom-call(bf16[1024,768]{1,0:T(8,128)(2,1)} %x_ref.1, s32[8,128]{1,0:T(8,128)} %bitcast.4, s32[8,128]{1,0:T(8,128)} %bitcast.5), custom_call_target="tpu_custom_call" | custom-call | tf_op jit(solution)/shard_map/pallas_call | solution.py:702
  46.3 0.6 %copy.5 = f32[1024]{0:T(1024)} copy(f32[1024]{0:T(1024)S(1)} %bitcast.3) | data formatting | bytes 8192

commit v9 on v7

--- a/solution.py
+++ b/solution.py
@@ -551,6 +551,17 @@
         def _():
             send(B, t).wait_recv()
 
+        @pl.when(up_r)
+        def _():
+            whole(B, order(B, t, chunks), 1, C, s_b, 4)
+
+        @pl.when(up_r & (i == chunks - 1))
+        def _():
+            for tile in range(chunks):
+                msg[2, tile:tile + 1, :] = jnp.maximum(
+                    msg[2, tile:tile + 1, :], masked(C, tile, s_b, qacc[4, :, part(tile)]))
+            message(2, above).start()
+
         @pl.when(has_a & comes)
         def _():
             some(B, order(B, t, chunks), 1, A, range(1), s_b, 3)
@@ -577,12 +588,12 @@
             def _():
                 message(0, second).start()
 
+        @pl.when(even & has_b & jnp.logical_not(up_r))
+        def _():
+            whole(B, order(B, t, chunks), 1, C, s_b, 4)
+
         @pl.when(even & has_b)
         def _():
-            whole(B, order(B, t, chunks), 1, C, s_b, 4)
-
-        @pl.when(even & has_b)
-        def _():
             message_b(order(B, t, chunks))
 
         return 0
@@ -593,7 +604,7 @@
     def _():
         message(1, first).start()
 
-    @pl.when(even)
+    @pl.when(even & jnp.logical_not(up_r))
     def _():
         for tile in range(chunks):
             msg[2, tile:tile + 1, :] = jnp.maximum(

time: 47.1 us -> 47.1 us (level)
  no operation moved by 1% of the time
where the time goes in v9:
time: 47.1 us; the launch traced here: 46.9 us
  Pallas kernels  46.3 us (98%)
  local copies, waits for them, and re-layouts  0.6 us (1%)
    pallas_call x1, Pallas kernels, shards(): pl.pallas_call(functools.partial(kernel, n_slab, n_member), out_shape=jax...  46.3 us

profile of v9, /device:TPU:7, one launch (start us, length us, event | category | flops | bytes accessed | tf_op | source)
XLA Modules:
  0.0 46.9 jit_solution(10265327400629615434)
XLA Ops:
  0.0 46.3 %shard_map.37 = f32[8,128]{1,0:T(8,128)S(1)} custom-call(bf16[1024,768]{1,0:T(8,128)(2,1)} %x_ref.1, s32[8,128]{1,0:T(8,128)} %bitcast.4, s32[8,128]{1,0:T(8,128)} %bitcast.5), custom_call_target="tpu_custom_call" | custom-call | tf_op jit(solution)/shard_map/pallas_call | solution.py:706
  46.3 0.6 %copy.5 = f32[1024]{0:T(1024)} copy(f32[1024]{0:T(1024)S(1)} %bitcast.3) | data formatting | bytes 8192
